TPU v7x, 512 devices: a whole 4x4x16 slice. The times are simulated.
512 devices in a mesh: group: 16 (over y, z_hi), expert: 32 (over x, z_lo, core).
Axes of the slice: x: 4, y: 4, z: 16 (z_hi: 4, z_lo: 4; z = z_hi * 4 + z_lo), core: 2. Of those that a mesh axis runs over, the one named last changes fastest.
Arguments:
- patches: bfloat16 [131072, 640], P(('group', 'expert')), may hold values from -8 to 8
- slot_params: bfloat16 [640, 256], replicated, may hold values from -5 to 5
- up_weight: bfloat16 [32, 640, 2560], P('expert', None, 'group'), may hold values from -0.25 to 0.25
- down_weight: bfloat16 [32, 2560, 640], P('expert', 'group'), may hold values from -0.125 to 0.125
- output_grad: bfloat16 [131072, 640], P(('group', 'expert')), may hold values from -6 to 6
Outputs:
- input_grad: bfloat16 [131072, 640], P(('group', 'expert'))
- slot_params_grad: float32 [640, 256], replicated
- up_grad: bfloat16 [32, 640, 2560], P('expert', 'group')
All inputs are finite; a program needn't handle non-finite values.
Results may differ from a plain program's by a relative error of at most 0.018.
Values may be sent and summed in bfloat16 or wider, within the bound.
No kernel may reach another device: no remote copies, remote signals or barrier semaphores. Data moves between devices by JAX's collectives and lax.ppermute only.
A program may use at most 64 MiB of HBM per device.

v0:
```python
import jax
import jax.numpy as jnp
from jax import lax
from jax.sharding import PartitionSpec as P

PATCHES = 256
SLOT_EXP = 8


cubic_coef = 0.044715
sqrt_ratio = 0.7978845608028654


def gelu_value(values):
    inner = sqrt_ratio * (values + cubic_coef * values * values * values)
    return 0.5 * values * (1.0 + jnp.tanh(inner))


def gelu_slope(values):
    tangent = jnp.tanh(sqrt_ratio * (values + cubic_coef * values * values * values))
    return 0.5 * (1.0 + tangent) + 0.5 * values * (1.0 - tangent * tangent) * sqrt_ratio * (
        1.0 + 3.0 * cubic_coef * values * values
    )


def local(patches, slot_params, up_weight, down_weight, output_grad):
    feature_width = patches.shape[1]
    images = patches.shape[0] // PATCHES
    owners = lax.axis_size("expert")
    local_experts = up_weight.shape[0]
    local_slots = local_experts * SLOT_EXP
    image_rows = patches.reshape(images, PATCHES, feature_width)
    grad_rows = output_grad.reshape(images, PATCHES, feature_width)
    logits = jnp.einsum("ipd,dn->ipn", image_rows, slot_params, preferred_element_type=jnp.float32)
    dispatch = jax.nn.softmax(logits, axis=1)
    combine = jax.nn.softmax(logits, axis=2)
    dispatch_low = dispatch.astype(jnp.bfloat16)
    combine_low = combine.astype(jnp.bfloat16)
    slots_in = jnp.einsum(
        "ipn,ipd->ind", dispatch_low, image_rows, preferred_element_type=jnp.float32
    ).astype(jnp.bfloat16)
    slot_grads = jnp.einsum(
        "ipn,ipd->ind", combine_low, grad_rows, preferred_element_type=jnp.float32
    ).astype(jnp.bfloat16)

    def outgoing(values):
        return values.reshape(images, owners, local_slots, feature_width)

    def landed(values):
        return values.reshape(images, owners * local_slots, feature_width)

    up_full = lax.all_gather(up_weight, "group", axis=2, tiled=True)
    down_full = lax.all_gather(down_weight, "group", axis=1, tiled=True)
    rows_in = lax.all_to_all(outgoing(slots_in), "expert", split_axis=1, concat_axis=0, tiled=True)
    hidden = jnp.einsum("resd,edf->resf", rows_in, up_full, preferred_element_type=jnp.float32)
    activation = gelu_value(hidden).astype(jnp.bfloat16)
    hidden, expert_out = (
        hidden,
        jnp.einsum(
            "resf,efd->resd", activation, down_full, preferred_element_type=jnp.float32
        ).astype(jnp.bfloat16),
    )
    slot_out = landed(lax.all_to_all(expert_out, "expert", split_axis=0, concat_axis=2, tiled=True))
    grads_in = lax.all_to_all(
        outgoing(slot_grads), "expert", split_axis=1, concat_axis=0, tiled=True
    )
    act_grad = jnp.einsum("resd,efd->resf", grads_in, down_full, preferred_element_type=jnp.float32)
    backward_hidden_grad = (act_grad * gelu_slope(hidden)).astype(jnp.bfloat16)
    rows_grad = jnp.einsum(
        "resf,edf->resd", backward_hidden_grad, up_full, preferred_element_type=jnp.float32
    ).astype(jnp.bfloat16)
    slot_in_grad = landed(
        lax.all_to_all(rows_grad, "expert", split_axis=0, concat_axis=2, tiled=True)
    )
    summed = lax.psum_scatter(
        jnp.einsum(
            "resd,resf->def", rows_in, backward_hidden_grad, preferred_element_type=jnp.float32
        ).astype(jnp.bfloat16),
        "group",
        scatter_dimension=0,
        tiled=True,
    ).astype(jnp.float32)
    up_grad = jnp.transpose(summed, (1, 0, 2)).astype(jnp.bfloat16)
    dcombine = jnp.einsum("ipd,ind->ipn", grad_rows, slot_out, preferred_element_type=jnp.float32)
    ddispatch = jnp.einsum(
        "ipd,ind->ipn", image_rows, slot_in_grad, preferred_element_type=jnp.float32
    )
    logit_grad = dispatch * (ddispatch - jnp.sum(dispatch * ddispatch, axis=1, keepdims=True))
    logit_grad = logit_grad + combine * (
        dcombine - jnp.sum(combine * dcombine, axis=2, keepdims=True)
    )
    logit_low = logit_grad.astype(jnp.bfloat16)
    image_grad = jnp.einsum(
        "ipn,ind->ipd", dispatch_low, slot_in_grad, preferred_element_type=jnp.float32
    )
    image_grad = image_grad + jnp.einsum(
        "ipn,dn->ipd", logit_low, slot_params, preferred_element_type=jnp.float32
    )
    phi_term = jnp.einsum("ipd,ipn->dn", image_rows, logit_low, preferred_element_type=jnp.float32)
    phi_grad = lax.psum(phi_term, ("group", "expert"))
    return (
        image_grad.astype(jnp.bfloat16).reshape(images * PATCHES, feature_width),
        phi_grad,
        up_grad,
    )


def solution(mesh):
    placed = (
        P(("group", "expert"), None),
        P(),
        P("expert", None, "group"),
        P("expert", "group", None),
        P(("group", "expert"), None),
    )
    return jax.shard_map(
        local,
        mesh=mesh,
        in_specs=placed,
        out_specs=(P(("group", "expert"), None), P(), P("expert", "group", None)),
        check_vma=False,
    )
```

profile of v0, /device:TPU:1, one launch (start us, length us, event | category | flops | bytes accessed | tf_op | source)
XLA Modules:
  0.0 1356.0 jit_solution(11212933343363887005)
XLA Ops:
  8.7 1.3 fusion.59
  11.2 10.4 all-to-all-start.1
  21.7 1.2 fusion.28
  22.8 11.6 all-to-all-done.1
  34.4 4.4 all-to-all-start
  38.8 96.7 %all-gather.5.cloned.1.call-done = bf16[1,640,2560]{1,2,0:T(8,128)(2,1)} async-done(((bf16[1,640,160]{1,2,0:T(8,128)(2,1)}), bf16[1,640,2560]{1,2,0:T(8,128)(2,1)}) %all-gather.5.cloned.1.call-update) | async-done | bytes 3276816 | tf_op jit(solution)/shard_map/all_gather | solution.py:52
  135.5 3.1 convolution_bitcast_fusion
  138.7 112.5 %all-gather.3.cloned.1.call-done = bf16[1,2560,640]{2,1,0:T(8,128)(2,1)} async-done(((bf16[1,160,640]{2,1,0:T(8,128)(2,1)}), bf16[1,2560,640]{2,1,0:T(8,128)(2,1)}) %all-gather.3.cloned.1.call-update) | async-done | bytes 3276816 | tf_op jit(solution)/shard_map/all_gather | solution.py:53
  251.2 4.3 fusion.33
  255.4 5.8 all-to-all-start.3
  261.2 4.2 fusion.3
  266.5 1.9 fusion.30
  268.4 5.5 all-to-all-done.3
  273.9 3.7 all-to-all-start.2
  277.7 1.3 convolution_bitcast_fusion.3
  279.0 11.4 all-to-all-done.2
  290.8 1.1 convolution_bitcast_fusion.2
  292.2 3.0 fusion
  295.2 14.0 %copy.30 = bf16[640,1,2560]{2,1,0:T(2,128)(2,1)} copy(bf16[640,1,2560]{0,2,1:T(8,128)(2,1)} %fusion) | data formatting | bytes 6553600 | tf_op jit(solution)/shard_map/convert_element_type | solution.py:78
  309.2 1.3 dynamic-slice
  312.5 436.3 %all-reduce.4.cloned.1.call-done = f32[640,256]{0,1:T(8,128)} async-done(((f32[640,256]{0,1:T(8,128)}), f32[640,256]{0,1:T(8,128)}) %all-reduce.4.cloned.1.call-update) | async-done | bytes 655376 | tf_op jit(solution)/shard_map/psum | solution.py:100
  748.7 2.2 copy.31
  750.9 596.4 %all-reduce.6.cloned.1.call-done = bf16[640,1,2560]{2,1,0:T(2,128)(2,1)} async-done(((bf16[640,1,2560]{2,1,0:T(2,128)(2,1)}), bf16[640,1,2560]{2,1,0:T(2,128)(2,1)}) %all-reduce.6.cloned.1.call-update) | async-done | bytes 3276816
  1347.3 1.4 constant_dynamic-slice_fusion
  (30 shorter events, 6.6 us)
Async XLA Ops:
  7.2 1.5 copy-start
  7.2 14.5 %copy-start.3 = (bf16[256,640]{1,0:T(8,128)(2,1)S(1)}, bf16[256,640]{1,0:T(8,128)(2,1)}, u32[]{:S(2)}) copy-start(bf16[256,640]{1,0:T(8,128)(2,1)} %param.9) | copy-start | bytes 983044
  7.2 128.4 %all-gather.5.cloned.1.call-start = ((), (), s32[]{:S(2)}) async-start(), calls=%async_computation.5 | async-start | bytes 3481600 | tf_op jit(solution)/shard_map/all_gather | solution.py:52
  7.9 243.2 %all-gather.3.cloned.1.call-start = ((), (), s32[]{:S(2)}) async-start(), calls=%async_computation.4 | async-start | bytes 3481600 | tf_op jit(solution)/shard_map/all_gather | solution.py:53
  11.2 23.2 %all-to-all-start.1 = ((bf16[1,32,8,640]{3,2,0,1:T(8,128)(2,1)}), bf16[1,32,8,640]{3,2,0,1:T(8,128)(2,1)S(1)}, u32[]{:S(2)}, u32[]{:S(2)}) async-start(bf16[1,32,8,640]{3,2,0,1:T(8,128)(2,1)} %fusion.29), calls=%async_computation.1 | async-start | bytes 655360 | tf_op jit(solution)/shard_map/all_to_all | solution.py:54
  34.4 221.0 %all-to-all-start = ((bf16[1,32,8,640]{3,2,0,1:T(8,128)(2,1)}), bf16[1,32,8,640]{3,2,0,1:T(8,128)(2,1)}, u32[]{:S(2)}, u32[]{:S(2)}) async-start(bf16[1,32,8,640]{3,2,0,1:T(8,128)(2,1)} %fusion.28), calls=%async_computation | async-start | bytes 655360 | tf_op jit(solution)/shard_map/all_to_all | solution.py:64
  255.4 18.5 %all-to-all-start.3 = ((bf16[32,1,8,640]{3,2,1,0:T(8,128)(2,1)}), bf16[32,1,8,640]{3,2,1,0:T(8,128)(2,1)}, u32[]{:S(2)}, u32[]{:S(2)}) async-start(bf16[32,1,8,640]{3,2,1,0:T(8,128)(2,1)} %fusion.33), calls=%async_computation.3 | async-start | bytes 655360 | tf_op jit(solution)/shard_map/all_to_all | solution.py:63
  261.2 5.3 copy-start.1
  265.4 1.1 copy-start.5
  266.5 11.1 copy-start.4
  273.9 16.4 %all-to-all-start.2 = ((bf16[32,1,8,640]{3,2,1,0:T(8,128)(2,1)}), bf16[32,1,8,640]{3,2,1,0:T(8,128)(2,1)S(1)}, u32[]{:S(2)}, u32[]{:S(2)}) async-start(bf16[32,1,8,640]{3,2,1,0:T(8,128)(2,1)} %fusion.30), calls=%async_computation.2 | async-start | bytes 655360 | tf_op jit(solution)/shard_map/all_to_all | solution.py:73
  277.6 471.1 %all-reduce.4.cloned.1.call-start = ((), (), s32[]{:S(2)}) async-start(), calls=%async_computation.6 | async-start | bytes 1310720 | tf_op jit(solution)/shard_map/psum | solution.py:100
  278.9 13.3 copy-start.6
  292.0 1055.3 %all-reduce.6.cloned.1.call-start = ((), (), s32[]{:S(2)}) async-start(), calls=%async_computation.7 | async-start | bytes 13107200
  309.2 2.3 copy-start.2
Sparse Core Ops, SparseCore 0:
  11.1 124.4 all-gather.4
  138.6 112.5 all-gather.2
  292.1 456.5 all-reduce.3
  751.8 595.4 all-reduce.5
where the time goes:
time: 1360 us
  waiting for transfers between devices  1270 us (93%)
  starting transfers between devices  24.6 us (2%)
  matrix products  24 us (2%)
  local copies, waits for them, and re-layouts  20.6 us (2%)
  between operations  14.6 us (1%)
    unnamed x5, waiting for transfers between devices  598 us
    psum x1, waiting for transfers between devices, local(): phi_grad = lax.psum(phi_term, ('group', 'expert'))  436 us
    all_gather x1, waiting for transfers between devices, local(): down_full = lax.all_gather(down_weight, 'group', axis=1, tiled=True)  112 us
    all_gather x1, waiting for transfers between devices, local(): up_full = lax.all_gather(up_weight, 'group', axis=2, tiled=True)  96.7 us
  transfers between devices with their start and end apart: 8, of which 7 were waited for; matrix products, arithmetic and copies ran while one was open for 3% of the time, Pallas kernels for 0%

commit v1 on v0

v1 whole, which is shorter than its diff:
```python
import jax
import jax.numpy as jnp
from jax import lax
from jax.sharding import Mesh, PartitionSpec as P

SLOT_EXP = 8
SIZES = {"y": 4, "h": 4, "x": 4, "l": 4, "c": 2}
AXES = ("y", "h", "x", "l", "c")
OWNERS = ("x", "l", "c")

cubic_coef = 0.044715
sqrt_ratio = 0.7978845608028654


def gelu_value(values):
    inner = sqrt_ratio * (values + cubic_coef * values * values * values)
    return 0.5 * values * (1.0 + jnp.tanh(inner))


def gelu_slope(values):
    tangent = jnp.tanh(sqrt_ratio * (values + cubic_coef * values * values * values))
    return 0.5 * (1.0 + tangent) + 0.5 * values * (1.0 - tangent * tangent) * sqrt_ratio * (
        1.0 + 3.0 * cubic_coef * values * values
    )


def mul(a, b, dims):
    return lax.dot_general(a, b, (dims, ((), ())), preferred_element_type=jnp.float32)


def shift(values, axis, step):
    size = lax.axis_size(axis)
    return lax.ppermute(values, axis, [(i, (i + step) % size) for i in range(size)])


def gather_hidden(weights):
    here = lax.axis_index("h")
    low = shift(weights, "h", 1)
    high = shift(weights, "h", -1)
    up_far = shift(low[0], "h", 1)
    down_far = shift(high[1], "h", -1)
    far = jnp.stack([up_far, down_far])
    full = jnp.zeros((2, 4) + weights.shape[1:], weights.dtype)
    for block, offset in ((weights, 0), (low, 3), (high, 1), (far, 2)):
        full = lax.dynamic_update_slice_in_dim(full, block[:, None], (here + offset) % 4, 1)
    return full


def everywhere(values, axes, count):
    spread = jnp.broadcast_to(values[None], (count,) + values.shape)
    return lax.all_to_all(spread, axes, 0, 0)


def local(patches, slot_params, up_weight, down_weight, output_grad):
    width = patches.shape[1]
    slots = slot_params.shape[1]
    owners = slots // SLOT_EXP
    shard = up_weight.shape[2]
    low = jnp.bfloat16

    weights = jnp.stack([up_weight[0].T, down_weight[0]])
    full = gather_hidden(weights).reshape(2, 4 * shard, width)
    up_rows, down_rows = full[0], full[1]

    logits = mul(patches, slot_params, ((1,), (0,)))
    dispatch = jax.nn.softmax(logits, axis=0)
    combine = jax.nn.softmax(logits, axis=1)
    dispatch_low = dispatch.astype(low)
    combine_low = combine.astype(low)
    slots_in = mul(dispatch_low, patches, ((0,), (0,))).astype(low)
    slot_grads = mul(combine_low, output_grad, ((0,), (0,))).astype(low)

    both = jnp.stack([slots_in, slot_grads]).reshape(2, owners, SLOT_EXP, width)
    landed = lax.all_to_all(both, OWNERS, 1, 1, tiled=True).reshape(2, slots, width)
    rows = everywhere(landed, "y", 4)
    rows_in = rows[:, 0].reshape(4 * slots, width)
    grads_in = rows[:, 1].reshape(4 * slots, width)

    hidden = mul(rows_in, up_rows, ((1,), (1,)))
    act_grad = mul(grads_in, down_rows, ((1,), (1,)))
    activation = gelu_value(hidden).astype(low)
    hidden_grad = (act_grad * gelu_slope(hidden)).astype(low)
    part_out = mul(activation, down_rows, ((1,), (0,))).astype(low)
    part_in = mul(hidden_grad, up_rows, ((1,), (0,))).astype(low)
    parts = jnp.stack([part_out.reshape(4, slots, width), part_in.reshape(4, slots, width)], axis=1)
    summed = jnp.sum(lax.all_to_all(parts, "y", 0, 0).astype(jnp.float32), axis=0).astype(low)
    back = lax.all_to_all(
        summed.reshape(2, owners, SLOT_EXP, width), OWNERS, 1, 1, tiled=True
    ).reshape(2, slots, width)
    slot_out, slot_in_grad = back[0], back[1]

    up_term = mul(rows_in, hidden_grad, ((0,), (0,))).astype(low)
    up_term = up_term.reshape(4, 4, width // 16, 4 * shard)
    up_term = lax.all_to_all(up_term, "h", 1, 0)
    up_sum = jnp.sum(up_term.astype(jnp.float32), axis=0).astype(low)
    up_grad = lax.all_to_all(up_sum, "y", 0, 0)
    up_grad = jnp.transpose(up_grad, (1, 0, 2)).reshape(1, width // 16, 16 * shard)

    dcombine = mul(output_grad, slot_out, ((1,), (1,)))
    ddispatch = mul(patches, slot_in_grad, ((1,), (1,)))
    logit_grad = dispatch * (ddispatch - jnp.sum(dispatch * ddispatch, axis=0, keepdims=True))
    logit_grad = logit_grad + combine * (
        dcombine - jnp.sum(combine * dcombine, axis=1, keepdims=True)
    )
    logit_low = logit_grad.astype(low)

    phi_term = mul(patches, logit_low, ((0,), (0,))).astype(low)
    pieces = SIZES["y"] * SIZES["x"] * SIZES["c"]
    piece = phi_term.reshape(pieces, width // pieces, slots)
    piece = jnp.sum(lax.all_to_all(piece, ("y", "x", "c"), 0, 0).astype(jnp.float32), axis=0)
    piece = everywhere(piece.astype(low), ("h", "l"), SIZES["h"] * SIZES["l"])
    piece = jnp.sum(piece.astype(jnp.float32), axis=0)
    phi_grad = everywhere(piece.astype(low), ("y", "x", "c"), pieces)
    phi_grad = phi_grad.reshape(width, slots).astype(jnp.float32)

    image_grad = mul(dispatch_low, slot_in_grad, ((1,), (0,)))
    image_grad = image_grad + mul(logit_low, slot_params, ((1,), (1,)))
    return image_grad.astype(low), phi_grad, up_grad


def solution(mesh):
    fine = Mesh(mesh.devices.reshape([SIZES[name] for name in AXES]), AXES)
    group = ("y", "h")
    placed = (
        P(AXES, None),
        P(),
        P(OWNERS, None, group),
        P(OWNERS, group, None),
        P(AXES, None),
    )
    return jax.shard_map(
        local,
        mesh=fine,
        in_specs=placed,
        out_specs=(P(AXES, None), P(), P(OWNERS, group, None)),
        check_vma=False,
    )
```

time: 1360 us -> 301 us (0.22)
  waiting for transfers between devices: 1270 us -> 132 us
  blocking collectives: 0 us -> 64.2 us
  starting transfers between devices: 24.6 us -> 64.9 us
  between operations: 14.6 us -> 1 us
    unnamed x5 -> x0, waiting for transfers between devices: 598 us -> none
    psum x1 -> x0, waiting for transfers between devices: 436 us -> none  [local(): phi_grad = lax.psum(phi_term, ('group', 'expert'))]
    all_gather x2 -> x0, waiting for transfers between devices: 209 us -> none  [the longest x1 112 us: local(): down_full = lax.all_gather(down_weight, 'group', axis=1, tiled=True)]
    all_to_all x0 -> x2, blocking collectives: none -> 64.2 us  [the longest x1 34.9 us: local(): lax.all_to_all(parts, 'y', 0, 0).astype(jnp.float32)]
    all_to_all x4 -> x7, waiting for transfers between devices: 28.5 us -> 89 us  [the longest x1 37.8 us: local(): up_term = lax.all_to_all(up_term, 'h', 1, 0)]
    ppermute x0 -> x4, waiting for transfers between devices: none -> 43.4 us  [shift(): lax.ppermute(values, axis, [(i, (i + step) % size) for i in range(size)])]
    ppermute x0 -> x4, starting transfers between devices: none -> 22.2 us  [shift(): lax.ppermute(values, axis, [(i, (i + step) % size) for i in range(size)])]
    all_to_all x4 -> x7, starting transfers between devices: 24.2 us -> 42.7 us  [the longest x3 17.1 us: everywhere(): return lax.all_to_all(spread, axes, 0, 0)]
  transfers between devices with their start and end apart: 8 -> 11, of which waited for: 7 -> 10; matrix products, arithmetic and copies ran while one was open for 3% -> 6% of each run, Pallas kernels for 0% -> 0%
where the time goes in v1:
time: 301 us; the launch traced here: 299 us
  waiting for transfers between devices  132 us (44%)
  starting transfers between devices  64.9 us (22%)
  blocking collectives  64.2 us (21%)
  local copies, waits for them, and re-layouts  16.6 us (6%)
  matrix products  14.4 us (5%)
  other arithmetic  5.85 us (2%)
    ppermute x4, waiting for transfers between devices, shift(): lax.ppermute(values, axis, [(i, (i + step) % size) for i in range(size)])  43.4 us
    all_to_all x1, waiting for transfers between devices, local(): up_term = lax.all_to_all(up_term, 'h', 1, 0)  37.8 us
    all_to_all x1, blocking collectives, local(): lax.all_to_all(parts, 'y', 0, 0).astype(jnp.float32)  34.9 us
    all_to_all x1, blocking collectives, local(): lax.all_to_all(both, OWNERS, 1, 1, tiled=True).reshape(2, slots, width)  29.4 us
    ppermute x4, starting transfers between devices, shift(): lax.ppermute(values, axis, [(i, (i + step) % size) for i in range(size)])  22.2 us
    all_to_all x3, waiting for transfers between devices, everywhere(): return lax.all_to_all(spread, axes, 0, 0)  20.4 us
    all_to_all x3, starting transfers between devices, everywhere(): return lax.all_to_all(spread, axes, 0, 0)  17.1 us
    all_to_all x1, waiting for transfers between devices, local(): lax.all_to_all(summed.reshape(2, owners, SLOT_EXP, width), OWNERS, 1, 1,...  16 us
  transfers between devices with their start and end apart: 11, of which 10 were waited for; matrix products, arithmetic and copies ran while one was open for 6% of the time, Pallas kernels for 0%

profile of v1, /device:TPU:1, one launch (start us, length us, event | category | flops | bytes accessed | tf_op | source)
XLA Modules:
  0.0 299.3 jit_solution(8844930074908486386)
XLA Ops:
  4.9 29.4 %all_to_all.49 = bf16[2,32,8,640]{3,2,0,1:T(8,128)(2,1)S(1)} all-to-all(bf16[2,32,8,640]{3,2,0,1:T(8,128)(2,1)S(1)} %pad_maximum_fusion.1), channel_id=1, replica_groups=mesh['y'=4,'h'=4,'x'=4,'l'=4,'c'=2] {'x','l','c'}, dimensions={1} | all-to-all | bytes 1310720 | tf_op jit(solution)/shard_map/all_to_all | solution.py:74
  36.1 4.3 %all-to-all-start.1 = ((bf16[4,2,256,640]{3,2,1,0:T(8,128)(2,1)}), bf16[4,2,256,640]{3,2,1,0:T(8,128)(2,1)S(1)}, u32[]{:S(2)}, u32[]{:S(2)}) async-start(bf16[4,2,256,640]{3,2,1,0:T(8,128)(2,1)} %broadcast_in_dim.19), calls=%async_computation.1 | async-start | bytes 5242880 | tf_op jit(solution)/shard_map/all_to_all | solution.py:51
  42.2 8.8 %collective-permute-start = (bf16[2,160,640]{2,1,0:T(8,128)(2,1)}, bf16[2,160,640]{2,1,0:T(8,128)(2,1)}, u32[]{:S(2)}, u32[]{:S(2)}) collective-permute-start(bf16[2,160,640]{2,1,0:T(8,128)(2,1)} %pad_maximum_fusion.2), channel_id=1, source_target_pairs={{0,32},{32,64},{64,96},{96,0},{1,33},{33,65},{65,97},{97,1},{2,34}... | collective-permute-start | bytes 1228808 | tf_op jit(solution)/shard_map/ppermute | solution.py:33
  51.0 2.9 collective-permute-start.1
  55.0 29.2 %collective-permute-done = bf16[2,160,640]{2,1,0:T(8,128)(2,1)} collective-permute-done((bf16[2,160,640]{2,1,0:T(8,128)(2,1)}, bf16[2,160,640]{2,1,0:T(8,128)(2,1)}, u32[]{:S(2)}, u32[]{:S(2)}) %collective-permute-start) | collective-permute-done | bytes 409632 | tf_op jit(solution)/shard_map/ppermute | solution.py:33
  85.2 7.6 %collective-permute-start.2 = (bf16[160,640]{1,0:T(8,128)(2,1)S(1)}, bf16[160,640]{1,0:T(8,128)(2,1)S(1)}, u32[]{:S(2)}, u32[]{:S(2)}) collective-permute-start(bf16[160,640]{1,0:T(8,128)(2,1)S(1)} %slice_bitcast_fusion.6), channel_id=1, source_target_pairs={{0,32},{32,64},{64,96},{96,0},{1,33},{33,65},{65,97},{97,1},{2,34}... | collective-permute-start | bytes 614408 | tf_op jit(solution)/shard_map/ppermute | solution.py:33
  92.8 4.8 %collective-permute-done.1 = bf16[2,160,640]{2,1,0:T(8,128)(2,1)} collective-permute-done((bf16[2,160,640]{2,1,0:T(8,128)(2,1)}, bf16[2,160,640]{2,1,0:T(8,128)(2,1)}, u32[]{:S(2)}, u32[]{:S(2)}) %collective-permute-start.1) | collective-permute-done | bytes 409632 | tf_op jit(solution)/shard_map/ppermute | solution.py:33
  98.5 2.9 collective-permute-start.3
  103.6 7.5 %collective-permute-done.2 = bf16[160,640]{1,0:T(8,128)(2,1)S(1)} collective-permute-done((bf16[160,640]{1,0:T(8,128)(2,1)S(1)}, bf16[160,640]{1,0:T(8,128)(2,1)S(1)}, u32[]{:S(2)}, u32[]{:S(2)}) %collective-permute-start.2) | collective-permute-done | bytes 204832 | tf_op jit(solution)/shard_map/ppermute | solution.py:33
  118.4 2.4 fusion.6
  122.4 34.9 %all_to_all.50 = bf16[4,2,256,640]{3,2,1,0:T(8,128)(2,1)S(1)} all-to-all(bf16[4,2,256,640]{3,2,1,0:T(8,128)(2,1)S(1)} %pad_maximum_fusion), channel_id=1, replica_groups=mesh['y'=4,'h'=4,'x'=4,'l'=4,'c'=2] {'y'}, dimensions={0} | all-to-all | bytes 5242880 | tf_op jit(solution)/shard_map/all_to_all | solution.py:86
  160.8 9.3 %all-to-all-start.3 = ((bf16[2,32,8,640]{3,2,0,1:T(8,128)(2,1)}), bf16[2,32,8,640]{3,2,0,1:T(8,128)(2,1)S(1)}, u32[]{:S(2)}, u32[]{:S(2)}) async-start(bf16[2,32,8,640]{3,2,0,1:T(8,128)(2,1)} %copy.46), calls=%async_computation.3 | async-start | bytes 1310720 | tf_op jit(solution)/shard_map/all_to_all | solution.py:87
  170.1 2.5 convolution_convert_fusion.2
  173.6 16.0 %all-to-all-done.3 = bf16[2,32,8,640]{3,2,0,1:T(8,128)(2,1)S(1)} async-done(((bf16[2,32,8,640]{3,2,0,1:T(8,128)(2,1)}), bf16[2,32,8,640]{3,2,0,1:T(8,128)(2,1)S(1)}, u32[]{:S(2)}, u32[]{:S(2)}) %all-to-all-start.3) | async-done | bytes 655392 | tf_op jit(solution)/shard_map/all_to_all | solution.py:87
  189.7 5.1 %all-to-all-start.7 = ((bf16[1,4,4,40,640]{4,3,1,0,2:T(8,128)(2,1)}), bf16[1,4,4,40,640]{4,3,1,0,2:T(8,128)(2,1)S(1)}, u32[]{:S(2)}, u32[]{:S(2)}) async-start(bf16[1,4,4,40,640]{4,3,1,0,2:T(8,128)(2,1)} %copy.50), calls=%async_computation.7 | async-start | bytes 1638400 | tf_op jit(solution)/shard_map/all_to_all | solution.py:94
  196.8 37.8 %all-to-all-done.7 = bf16[1,4,4,40,640]{4,3,1,0,2:T(8,128)(2,1)S(1)} async-done(((bf16[1,4,4,40,640]{4,3,1,0,2:T(8,128)(2,1)}), bf16[1,4,4,40,640]{4,3,1,0,2:T(8,128)(2,1)S(1)}, u32[]{:S(2)}, u32[]{:S(2)}) %all-to-all-start.7) | async-done | bytes 819232 | tf_op jit(solution)/shard_map/all_to_all | solution.py:94
  234.6 7.8 %all-to-all-start.4 = ((bf16[32,20,256]{2,1,0:T(8,128)(2,1)}), bf16[32,20,256]{2,1,0:T(8,128)(2,1)S(1)}, u32[]{:S(2)}, u32[]{:S(2)}) async-start(bf16[32,20,256]{2,1,0:T(8,128)(2,1)} %reshape.44), calls=%async_computation.4 | async-start | bytes 786432 | tf_op jit(solution)/shard_map/all_to_all | solution.py:110
  243.3 9.3 %all-to-all-done.4 = bf16[32,20,256]{2,1,0:T(8,128)(2,1)S(1)} async-done(((bf16[32,20,256]{2,1,0:T(8,128)(2,1)}), bf16[32,20,256]{2,1,0:T(8,128)(2,1)S(1)}, u32[]{:S(2)}, u32[]{:S(2)}) %all-to-all-start.4) | async-done | bytes 327712 | tf_op jit(solution)/shard_map/all_to_all | solution.py:110
  252.6 3.4 %all-to-all-start.8 = ((bf16[4,40,640]{2,1,0:T(8,128)(2,1)}), bf16[4,40,640]{2,1,0:T(8,128)(2,1)S(1)}, u32[]{:S(2)}, u32[]{:S(2)}) async-start(bf16[4,40,640]{2,1,0:T(8,128)(2,1)} %reduce_sum.91), calls=%async_computation.8 | async-start | bytes 409600 | tf_op jit(solution)/shard_map/all_to_all | solution.py:96
  256.1 5.4 %all-to-all-done.8 = bf16[4,40,640]{2,1,0:T(8,128)(2,1)S(1)} async-done(((bf16[4,40,640]{2,1,0:T(8,128)(2,1)}), bf16[4,40,640]{2,1,0:T(8,128)(2,1)S(1)}, u32[]{:S(2)}, u32[]{:S(2)}) %all-to-all-start.8) | async-done | bytes 204832 | tf_op jit(solution)/shard_map/all_to_all | solution.py:96
  262.2 3.8 %all-to-all-start.5 = ((bf16[16,20,256]{2,1,0:T(8,128)(2,1)}), bf16[16,20,256]{2,1,0:T(8,128)(2,1)S(1)}, u32[]{:S(2)}, u32[]{:S(2)}) async-start(bf16[16,20,256]{2,1,0:T(8,128)(2,1)} %broadcast_in_dim.47), calls=%async_computation.5 | async-start | bytes 393216 | tf_op jit(solution)/shard_map/all_to_all | solution.py:51
  266.8 11.5 %all-to-all-done.5 = bf16[16,20,256]{2,1,0:T(8,128)(2,1)S(1)} async-done(((bf16[16,20,256]{2,1,0:T(8,128)(2,1)}), bf16[16,20,256]{2,1,0:T(8,128)(2,1)S(1)}, u32[]{:S(2)}, u32[]{:S(2)}) %all-to-all-start.5) | async-done | bytes 163872 | tf_op jit(solution)/shard_map/all_to_all | solution.py:51
  279.1 9.1 %all-to-all-start.6 = ((bf16[32,20,256]{2,1,0:T(8,128)(2,1)}), bf16[32,20,256]{2,1,0:T(8,128)(2,1)S(1)}, u32[]{:S(2)}, u32[]{:S(2)}) async-start(bf16[32,20,256]{2,1,0:T(8,128)(2,1)} %broadcast_in_dim.48), calls=%async_computation.6 | async-start | bytes 786432 | tf_op jit(solution)/shard_map/all_to_all | solution.py:51
  289.5 8.9 %all-to-all-done.6 = bf16[32,20,256]{2,1,0:T(8,128)(2,1)S(1)} async-done(((bf16[32,20,256]{2,1,0:T(8,128)(2,1)}), bf16[32,20,256]{2,1,0:T(8,128)(2,1)S(1)}, u32[]{:S(2)}, u32[]{:S(2)}) %all-to-all-start.6) | async-done | bytes 327712 | tf_op jit(solution)/shard_map/all_to_all | solution.py:51
  (60 shorter events, 33.8 us)
Async XLA Ops:
  0.6 1.0 copy-start
  36.1 4.3 %copy-start.6 = (bf16[1,160,640]{2,1,0:T(8,128)(2,1)S(1)}, bf16[1,160,640]{2,1,0:T(8,128)(2,1)}, u32[]{:S(2)}) copy-start(bf16[1,160,640]{2,1,0:T(8,128)(2,1)} %param.8) | copy-start | bytes 614404
  36.1 78.2 %all-to-all-start.1 = ((bf16[4,2,256,640]{3,2,1,0:T(8,128)(2,1)}), bf16[4,2,256,640]{3,2,1,0:T(8,128)(2,1)S(1)}, u32[]{:S(2)}, u32[]{:S(2)}) async-start(bf16[4,2,256,640]{3,2,1,0:T(8,128)(2,1)} %broadcast_in_dim.19), calls=%async_computation.1 | async-start | bytes 5242880 | tf_op jit(solution)/shard_map/all_to_all | solution.py:51
  42.2 42.1 %collective-permute-start = (bf16[2,160,640]{2,1,0:T(8,128)(2,1)}, bf16[2,160,640]{2,1,0:T(8,128)(2,1)}, u32[]{:S(2)}, u32[]{:S(2)}) collective-permute-start(bf16[2,160,640]{2,1,0:T(8,128)(2,1)} %pad_maximum_fusion.2), channel_id=1, source_target_pairs={{0,32},{32,64},{64,96},{96,0},{1,33},{33,65},{65,97},{97,1},{2,34}... | collective-permute-start | bytes 1228808 | tf_op jit(solution)/shard_map/ppermute | solution.py:33
  51.0 46.6 %collective-permute-start.1 = (bf16[2,160,640]{2,1,0:T(8,128)(2,1)}, bf16[2,160,640]{2,1,0:T(8,128)(2,1)}, u32[]{:S(2)}, u32[]{:S(2)}) collective-permute-start(bf16[2,160,640]{2,1,0:T(8,128)(2,1)} %pad_maximum_fusion.2), channel_id=1, source_target_pairs={{0,96},{32,0},{64,32},{96,64},{1,97},{33,1},{65,33},{97,65},{2,98}... | collective-permute-start | bytes 1228808 | tf_op jit(solution)/shard_map/ppermute | solution.py:33
  85.2 25.9 %collective-permute-start.2 = (bf16[160,640]{1,0:T(8,128)(2,1)S(1)}, bf16[160,640]{1,0:T(8,128)(2,1)S(1)}, u32[]{:S(2)}, u32[]{:S(2)}) collective-permute-start(bf16[160,640]{1,0:T(8,128)(2,1)S(1)} %slice_bitcast_fusion.6), channel_id=1, source_target_pairs={{0,32},{32,64},{64,96},{96,0},{1,33},{33,65},{65,97},{97,1},{2,34}... | collective-permute-start | bytes 614408 | tf_op jit(solution)/shard_map/ppermute | solution.py:33
  98.5 14.4 %collective-permute-start.3 = (bf16[160,640]{1,0:T(8,128)(2,1)S(1)}, bf16[160,640]{1,0:T(8,128)(2,1)S(1)}, u32[]{:S(2)}, u32[]{:S(2)}) collective-permute-start(bf16[160,640]{1,0:T(8,128)(2,1)S(1)} %slice_bitcast_fusion.5), channel_id=1, source_target_pairs={{0,96},{32,0},{64,32},{96,64},{1,97},{33,1},{65,33},{97,65},{2,98}... | collective-permute-start | bytes 614408 | tf_op jit(solution)/shard_map/ppermute | solution.py:33
  114.3 1.1 copy-start.4
  114.5 3.8 %copy-start.1 = (bf16[4,1,256,640]{3,2,1,0:T(8,128)(2,1)}, bf16[4,1,256,640]{3,2,1,0:T(8,128)(2,1)S(1)}, u32[]{:S(2)}) copy-start(bf16[4,1,256,640]{3,2,1,0:T(8,128)(2,1)S(1)} %get-tuple-element.10) | copy-start | bytes 3932164
  114.5 2.2 copy-start.5
  120.8 1.3 copy-start.8
  158.7 11.4 %copy-start.2 = (bf16[4,1,256,640]{3,2,1,0:T(8,128)(2,1)S(1)}, bf16[4,1,256,640]{3,2,1,0:T(8,128)(2,1)}, u32[]{:S(2)}) copy-start(bf16[4,1,256,640]{3,2,1,0:T(8,128)(2,1)} %copy-done.1) | copy-start | bytes 3932164
  160.8 28.9 %all-to-all-start.3 = ((bf16[2,32,8,640]{3,2,0,1:T(8,128)(2,1)}), bf16[2,32,8,640]{3,2,0,1:T(8,128)(2,1)S(1)}, u32[]{:S(2)}, u32[]{:S(2)}) async-start(bf16[2,32,8,640]{3,2,0,1:T(8,128)(2,1)} %copy.46), calls=%async_computation.3 | async-start | bytes 1310720 | tf_op jit(solution)/shard_map/all_to_all | solution.py:87
  172.6 22.1 %copy-start.7 = (bf16[256,640]{1,0:T(8,128)(2,1)S(1)}, bf16[256,640]{1,0:T(8,128)(2,1)}, u32[]{:S(2)}) copy-start(bf16[256,640]{1,0:T(8,128)(2,1)} %param.9) | copy-start | bytes 983044
  189.7 45.0 %all-to-all-start.7 = ((bf16[1,4,4,40,640]{4,3,1,0,2:T(8,128)(2,1)}), bf16[1,4,4,40,640]{4,3,1,0,2:T(8,128)(2,1)S(1)}, u32[]{:S(2)}, u32[]{:S(2)}) async-start(bf16[1,4,4,40,640]{4,3,1,0,2:T(8,128)(2,1)} %copy.50), calls=%async_computation.7 | async-start | bytes 1638400 | tf_op jit(solution)/shard_map/all_to_all | solution.py:94
  234.6 18.0 %all-to-all-start.4 = ((bf16[32,20,256]{2,1,0:T(8,128)(2,1)}), bf16[32,20,256]{2,1,0:T(8,128)(2,1)S(1)}, u32[]{:S(2)}, u32[]{:S(2)}) async-start(bf16[32,20,256]{2,1,0:T(8,128)(2,1)} %reshape.44), calls=%async_computation.4 | async-start | bytes 786432 | tf_op jit(solution)/shard_map/all_to_all | solution.py:110
  243.3 45.2 %copy-start.3 = (bf16[640,256]{1,0:T(8,128)(2,1)S(1)}, bf16[640,256]{1,0:T(8,128)(2,1)}, u32[]{:S(2)}) copy-start(bf16[640,256]{1,0:T(8,128)(2,1)} %param.6) | copy-start | bytes 983044
  252.6 8.9 %all-to-all-start.8 = ((bf16[4,40,640]{2,1,0:T(8,128)(2,1)}), bf16[4,40,640]{2,1,0:T(8,128)(2,1)S(1)}, u32[]{:S(2)}, u32[]{:S(2)}) async-start(bf16[4,40,640]{2,1,0:T(8,128)(2,1)} %reduce_sum.91), calls=%async_computation.8 | async-start | bytes 409600 | tf_op jit(solution)/shard_map/all_to_all | solution.py:96
  262.2 16.1 %all-to-all-start.5 = ((bf16[16,20,256]{2,1,0:T(8,128)(2,1)}), bf16[16,20,256]{2,1,0:T(8,128)(2,1)S(1)}, u32[]{:S(2)}, u32[]{:S(2)}) async-start(bf16[16,20,256]{2,1,0:T(8,128)(2,1)} %broadcast_in_dim.47), calls=%async_computation.5 | async-start | bytes 393216 | tf_op jit(solution)/shard_map/all_to_all | solution.py:51
  279.1 19.3 %all-to-all-start.6 = ((bf16[32,20,256]{2,1,0:T(8,128)(2,1)}), bf16[32,20,256]{2,1,0:T(8,128)(2,1)S(1)}, u32[]{:S(2)}, u32[]{:S(2)}) async-start(bf16[32,20,256]{2,1,0:T(8,128)(2,1)} %broadcast_in_dim.48), calls=%async_computation.6 | async-start | bytes 786432 | tf_op jit(solution)/shard_map/all_to_all | solution.py:51

commit v2 on v1

--- a/solution.py
+++ b/solution.py
@@ -33,10 +33,8 @@
     return lax.ppermute(values, axis, [(i, (i + step) % size) for i in range(size)])
 
 
-def gather_hidden(weights):
+def gather_hidden(weights, low, high):
     here = lax.axis_index("h")
-    low = shift(weights, "h", 1)
-    high = shift(weights, "h", -1)
     up_far = shift(low[0], "h", 1)
     down_far = shift(high[1], "h", -1)
     far = jnp.stack([up_far, down_far])
@@ -44,6 +42,24 @@
     for block, offset in ((weights, 0), (low, 3), (high, 1), (far, 2)):
         full = lax.dynamic_update_slice_in_dim(full, block[:, None], (here + offset) % 4, 1)
     return full
+
+
+def sum_hidden(terms):
+    here = lax.axis_index("h")
+
+    def chunk(offset):
+        return lax.dynamic_index_in_dim(terms, (here + offset) % 4, 1, keepdims=False)
+
+    def add(one, other):
+        return (one.astype(jnp.float32) + other.astype(jnp.float32)).astype(terms.dtype)
+
+    far, right, left = chunk(2), chunk(1), chunk(3)
+    far_right = shift(far[:2], "h", 1)
+    far_left = shift(far[2:], "h", -1)
+    right = shift(jnp.concatenate([add(right[:2], far_right), right[2:]]), "h", 1)
+    left = shift(jnp.concatenate([left[:2], add(left[2:], far_left)]), "h", -1)
+    total = chunk(0).astype(jnp.float32) + right.astype(jnp.float32) + left.astype(jnp.float32)
+    return total.astype(terms.dtype)
 
 
 def everywhere(values, axes, count):
@@ -59,8 +75,8 @@
     low = jnp.bfloat16
 
     weights = jnp.stack([up_weight[0].T, down_weight[0]])
-    full = gather_hidden(weights).reshape(2, 4 * shard, width)
-    up_rows, down_rows = full[0], full[1]
+    from_low = shift(weights, "h", 1)
+    from_high = shift(weights, "h", -1)
 
     logits = mul(patches, slot_params, ((1,), (0,)))
     dispatch = jax.nn.softmax(logits, axis=0)
@@ -72,6 +88,9 @@
 
     both = jnp.stack([slots_in, slot_grads]).reshape(2, owners, SLOT_EXP, width)
     landed = lax.all_to_all(both, OWNERS, 1, 1, tiled=True).reshape(2, slots, width)
+    landed, from_low, from_high = lax.optimization_barrier((landed, from_low, from_high))
+    full = gather_hidden(weights, from_low, from_high).reshape(2, 4 * shard, width)
+    up_rows, down_rows = full[0], full[1]
     rows = everywhere(landed, "y", 4)
     rows_in = rows[:, 0].reshape(4 * slots, width)
     grads_in = rows[:, 1].reshape(4 * slots, width)
@@ -91,8 +110,7 @@
 
     up_term = mul(rows_in, hidden_grad, ((0,), (0,))).astype(low)
     up_term = up_term.reshape(4, 4, width // 16, 4 * shard)
-    up_term = lax.all_to_all(up_term, "h", 1, 0)
-    up_sum = jnp.sum(up_term.astype(jnp.float32), axis=0).astype(low)
+    up_sum = sum_hidden(up_term)
     up_grad = lax.all_to_all(up_sum, "y", 0, 0)
     up_grad = jnp.transpose(up_grad, (1, 0, 2)).reshape(1, width // 16, 16 * shard)
 

time: 301 us -> 271 us (0.900)
  starting transfers between devices: 64.9 us -> 108 us
  waiting for transfers between devices: 132 us -> 94.7 us
  blocking collectives: 64.2 us -> 32.8 us
  local copies, waits for them, and re-layouts: 16.6 us -> 12.8 us
    all_to_all x1 -> x0, blocking collectives: 29.4 us -> none  [local(): lax.all_to_all(both, OWNERS, 1, 1, tiled=True).reshape(2, slots, width)]
    ppermute x4 -> x8, waiting for transfers between devices: 43.4 us -> 21.2 us  [shift(): lax.ppermute(values, axis, [(i, (i + step) % size) for i in range(size)])]
    ppermute x4 -> x8, starting transfers between devices: 22.2 us -> 41.5 us  [shift(): lax.ppermute(values, axis, [(i, (i + step) % size) for i in range(size)])]
    all_to_all x1, waiting for transfers between devices: 16 us -> 0.01 us  [local(): lax.all_to_all(summed.reshape(2, owners, SLOT_EXP, width), OWNERS, 1, 1,...]
    all_to_all x1, starting transfers between devices: 9.31 us -> 19.9 us  [local(): lax.all_to_all(summed.reshape(2, owners, SLOT_EXP, width), OWNERS, 1, 1,...]
    all_to_all x3, starting transfers between devices: 17.1 us -> 26.1 us  [everywhere(): return lax.all_to_all(spread, axes, 0, 0)]
    all_to_all x1, starting transfers between devices: 5.05 us -> 10.4 us  [local(): lax.all_to_all(both, OWNERS, 1, 1, tiled=True).reshape(2, slots, width)]
    all_to_all x3, waiting for transfers between devices: 20.4 us -> 24.7 us  [everywhere(): return lax.all_to_all(spread, axes, 0, 0)]
  transfers between devices with their start and end apart: 11 -> 15, of which waited for: 10 -> 9; matrix products, arithmetic and copies ran while one was open for 6% -> 5% of each run, Pallas kernels for 0% -> 0%
where the time goes in v2:
time: 271 us; the launch traced here: 270 us
  starting transfers between devices  108 us (40%)
  waiting for transfers between devices  94.7 us (35%)
  blocking collectives  32.8 us (12%)
  matrix products  14.4 us (5%)
  local copies, waits for them, and re-layouts  12.8 us (5%)
  other arithmetic  6.08 us (2%)
    ppermute x8, starting transfers between devices, shift(): lax.ppermute(values, axis, [(i, (i + step) % size) for i in range(size)])  41.5 us
    all_to_all x1, waiting for transfers between devices, local(): lax.all_to_all(both, OWNERS, 1, 1, tiled=True).reshape(2, slots, width)  34.9 us
    all_to_all x1, blocking collectives, local(): lax.all_to_all(parts, 'y', 0, 0).astype(jnp.float32)  32.8 us
    all_to_all x3, starting transfers between devices, everywhere(): return lax.all_to_all(spread, axes, 0, 0)  26.1 us
    all_to_all x3, waiting for transfers between devices, everywhere(): return lax.all_to_all(spread, axes, 0, 0)  24.7 us
    ppermute x8, waiting for transfers between devices, shift(): lax.ppermute(values, axis, [(i, (i + step) % size) for i in range(size)])  21.2 us
    all_to_all x1, starting transfers between devices, local(): lax.all_to_all(summed.reshape(2, owners, SLOT_EXP, width), OWNERS, 1, 1,...  19.9 us
    dot_general x13, matrix products, mul(): lax.dot_general(a, b, (dims, ((), ())), preferred_element_type=jnp.float32)  14.4 us
  transfers between devices with their start and end apart: 15, of which 9 were waited for; matrix products, arithmetic and copies ran while one was open for 5% of the time, Pallas kernels for 0%

profile of v2, /device:TPU:1, one launch (start us, length us, event | category | flops | bytes accessed | tf_op | source)
XLA Modules:
  0.0 269.9 jit_solution(8888078099630355132)
XLA Ops:
  5.8 10.4 %all-to-all-start = ((bf16[2,32,8,640]{3,2,0,1:T(8,128)(2,1)}), bf16[2,32,8,640]{3,2,0,1:T(8,128)(2,1)S(1)}, u32[]{:S(2)}, u32[]{:S(2)}) async-start(bf16[2,32,8,640]{3,2,0,1:T(8,128)(2,1)} %pad_maximum_fusion.1), calls=%async_computation | async-start | bytes 1310720 | tf_op jit(solution)/shard_map/all_to_all | solution.py:90
  16.3 8.4 %collective-permute-start = (bf16[2,160,640]{2,1,0:T(8,128)(2,1)S(1)}, bf16[2,160,640]{2,1,0:T(8,128)(2,1)S(1)}, u32[]{:S(2)}, u32[]{:S(2)}) collective-permute-start(bf16[2,160,640]{2,1,0:T(8,128)(2,1)S(1)} %pad_maximum_fusion.2), channel_id=1, source_target_pairs={{0,32},{32,64},{64,96},{96,0},{1,33},{33,65},{65,97},{97,1},{2,34}... | collective-permute-start | bytes 1228808 | tf_op jit(solution)/shard_map/ppermute | solution.py:33
  24.7 2.9 %collective-permute-start.1 = (bf16[2,160,640]{2,1,0:T(8,128)(2,1)S(1)}, bf16[2,160,640]{2,1,0:T(8,128)(2,1)S(1)}, u32[]{:S(2)}, u32[]{:S(2)}) collective-permute-start(bf16[2,160,640]{2,1,0:T(8,128)(2,1)S(1)} %pad_maximum_fusion.2), channel_id=1, source_target_pairs={{0,96},{32,0},{64,32},{96,64},{1,97},{33,1},{65,33},{97,65},{2,98}... | collective-permute-start | bytes 1228808 | tf_op jit(solution)/shard_map/ppermute | solution.py:33
  27.6 34.9 %all-to-all-done = bf16[2,32,8,640]{3,2,0,1:T(8,128)(2,1)S(1)} async-done(((bf16[2,32,8,640]{3,2,0,1:T(8,128)(2,1)}), bf16[2,32,8,640]{3,2,0,1:T(8,128)(2,1)S(1)}, u32[]{:S(2)}, u32[]{:S(2)}) %all-to-all-start) | async-done | bytes 655392 | tf_op jit(solution)/shard_map/all_to_all | solution.py:90
  64.3 3.7 %all-to-all-start.1 = ((bf16[4,2,256,640]{3,2,1,0:T(8,128)(2,1)}), bf16[4,2,256,640]{3,2,1,0:T(8,128)(2,1)S(1)}, u32[]{:S(2)}, u32[]{:S(2)}) async-start(bf16[4,2,256,640]{3,2,1,0:T(8,128)(2,1)} %broadcast_in_dim.16), calls=%async_computation.1 | async-start | bytes 5242880 | tf_op jit(solution)/shard_map/all_to_all | solution.py:67
  70.2 8.7 %collective-permute-start.2 = (bf16[160,640]{1,0:T(8,128)(2,1)S(1)}, bf16[160,640]{1,0:T(8,128)(2,1)S(1)}, u32[]{:S(2)}, u32[]{:S(2)}) collective-permute-start(bf16[160,640]{1,0:T(8,128)(2,1)S(1)} %slice_bitcast_fusion.6), channel_id=1, source_target_pairs={{0,32},{32,64},{64,96},{96,0},{1,33},{33,65},{65,97},{97,1},{2,34}... | collective-permute-start | bytes 614408 | tf_op jit(solution)/shard_map/ppermute | solution.py:33
  82.0 5.4 %collective-permute-done.2 = bf16[160,640]{1,0:T(8,128)(2,1)S(1)} collective-permute-done((bf16[160,640]{1,0:T(8,128)(2,1)S(1)}, bf16[160,640]{1,0:T(8,128)(2,1)S(1)}, u32[]{:S(2)}, u32[]{:S(2)}) %collective-permute-start.2) | collective-permute-done | bytes 204832 | tf_op jit(solution)/shard_map/ppermute | solution.py:33
  87.4 6.4 %collective-permute-done.3 = bf16[160,640]{1,0:T(8,128)(2,1)S(1)} collective-permute-done((bf16[160,640]{1,0:T(8,128)(2,1)S(1)}, bf16[160,640]{1,0:T(8,128)(2,1)S(1)}, u32[]{:S(2)}, u32[]{:S(2)}) %collective-permute-start.3) | collective-permute-done | bytes 204832 | tf_op jit(solution)/shard_map/ppermute | solution.py:33
  95.2 4.4 %all-to-all-done.1 = bf16[4,2,256,640]{3,2,1,0:T(8,128)(2,1)S(1)} async-done(((bf16[4,2,256,640]{3,2,1,0:T(8,128)(2,1)}), bf16[4,2,256,640]{3,2,1,0:T(8,128)(2,1)S(1)}, u32[]{:S(2)}, u32[]{:S(2)}) %all-to-all-start.1) | async-done | bytes 2621472 | tf_op jit(solution)/shard_map/all_to_all | solution.py:67
  107.7 32.8 %all_to_all.40 = bf16[4,2,256,640]{3,2,1,0:T(8,128)(2,1)S(1)} all-to-all(bf16[4,2,256,640]{3,2,1,0:T(8,128)(2,1)S(1)} %pad_maximum_fusion), channel_id=1, replica_groups=mesh['y'=4,'h'=4,'x'=4,'l'=4,'c'=2] {'y'}, dimensions={0} | all-to-all | bytes 5242880 | tf_op jit(solution)/shard_map/all_to_all | solution.py:105
  144.0 19.9 %all-to-all-start.3 = ((bf16[2,32,8,640]{3,2,0,1:T(8,128)(2,1)}), bf16[2,32,8,640]{3,2,0,1:T(8,128)(2,1)S(1)}, u32[]{:S(2)}, u32[]{:S(2)}) async-start(bf16[2,32,8,640]{3,2,0,1:T(8,128)(2,1)} %copy.63), calls=%async_computation.3 | async-start | bytes 1310720 | tf_op jit(solution)/shard_map/all_to_all | solution.py:106
  166.5 5.3 %collective-permute-start.4 = (bf16[2,40,640]{2,1,0:T(8,128)(2,1)S(1)}, bf16[2,40,640]{2,1,0:T(8,128)(2,1)S(1)}, u32[]{:S(2)}, u32[]{:S(2)}) collective-permute-start(bf16[2,40,640]{2,1,0:T(8,128)(2,1)S(1)} %get-tuple-element.21), channel_id=1, source_target_pairs={{0,32},{32,64},{64,96},{96,0},{1,33},{33,65},{65,97},{97,1},{2,34}... | collective-permute-start | bytes 307208 | tf_op jit(solution)/shard_map/ppermute | solution.py:33
  171.8 4.1 %collective-permute-start.6 = (bf16[2,40,640]{2,1,0:T(8,128)(2,1)S(1)}, bf16[2,40,640]{2,1,0:T(8,128)(2,1)S(1)}, u32[]{:S(2)}, u32[]{:S(2)}) collective-permute-start(bf16[2,40,640]{2,1,0:T(8,128)(2,1)S(1)} %get-tuple-element.23), channel_id=1, source_target_pairs={{0,96},{32,0},{64,32},{96,64},{1,97},{33,1},{65,33},{97,65},{2,98}... | collective-permute-start | bytes 307208 | tf_op jit(solution)/shard_map/ppermute | solution.py:33
  175.9 9.4 %collective-permute-done.4 = bf16[2,40,640]{2,1,0:T(8,128)(2,1)S(1)} collective-permute-done((bf16[2,40,640]{2,1,0:T(8,128)(2,1)S(1)}, bf16[2,40,640]{2,1,0:T(8,128)(2,1)S(1)}, u32[]{:S(2)}, u32[]{:S(2)}) %collective-permute-start.4) | collective-permute-done | bytes 102432 | tf_op jit(solution)/shard_map/ppermute | solution.py:33
  185.4 4.0 %collective-permute-start.5 = (bf16[4,40,640]{2,1,0:T(8,128)(2,1)S(1)}, bf16[4,40,640]{2,1,0:T(8,128)(2,1)S(1)}, u32[]{:S(2)}, u32[]{:S(2)}) collective-permute-start(bf16[4,40,640]{2,1,0:T(8,128)(2,1)S(1)} %pad_maximum_fusion.3), channel_id=1, source_target_pairs={{0,32},{32,64},{64,96},{96,0},{1,33},{33,65},{65,97},{97,1},{2,34}... | collective-permute-start | bytes 614408 | tf_op jit(solution)/shard_map/ppermute | solution.py:33
  189.5 5.4 %collective-permute-start.7 = (bf16[4,40,640]{2,1,0:T(8,128)(2,1)S(1)}, bf16[4,40,640]{2,1,0:T(8,128)(2,1)S(1)}, u32[]{:S(2)}, u32[]{:S(2)}) collective-permute-start(bf16[4,40,640]{2,1,0:T(8,128)(2,1)S(1)} %pad_maximum_fusion.4), channel_id=1, source_target_pairs={{0,96},{32,0},{64,32},{96,64},{1,97},{33,1},{65,33},{97,65},{2,98}... | collective-permute-start | bytes 614408 | tf_op jit(solution)/shard_map/ppermute | solution.py:33
  197.0 6.5 %all-to-all-start.4 = ((bf16[32,20,256]{2,1,0:T(8,128)(2,1)}), bf16[32,20,256]{2,1,0:T(8,128)(2,1)S(1)}, u32[]{:S(2)}, u32[]{:S(2)}) async-start(bf16[32,20,256]{2,1,0:T(8,128)(2,1)} %reshape.62), calls=%async_computation.4 | async-start | bytes 786432 | tf_op jit(solution)/shard_map/all_to_all | solution.py:128
  205.2 8.5 %all-to-all-done.4 = bf16[32,20,256]{2,1,0:T(8,128)(2,1)S(1)} async-done(((bf16[32,20,256]{2,1,0:T(8,128)(2,1)}), bf16[32,20,256]{2,1,0:T(8,128)(2,1)S(1)}, u32[]{:S(2)}, u32[]{:S(2)}) %all-to-all-start.4) | async-done | bytes 327712 | tf_op jit(solution)/shard_map/all_to_all | solution.py:128
  213.6 3.4 %all-to-all-start.7 = ((bf16[4,40,640]{2,1,0:T(8,128)(2,1)}), bf16[4,40,640]{2,1,0:T(8,128)(2,1)S(1)}, u32[]{:S(2)}, u32[]{:S(2)}) async-start(bf16[4,40,640]{2,1,0:T(8,128)(2,1)} %fusion.17), calls=%async_computation.7 | async-start | bytes 409600 | tf_op jit(solution)/shard_map/all_to_all | solution.py:114
  217.1 5.4 %all-to-all-done.7 = bf16[4,40,640]{2,1,0:T(8,128)(2,1)S(1)} async-done(((bf16[4,40,640]{2,1,0:T(8,128)(2,1)}), bf16[4,40,640]{2,1,0:T(8,128)(2,1)S(1)}, u32[]{:S(2)}, u32[]{:S(2)}) %all-to-all-start.7) | async-done | bytes 204832 | tf_op jit(solution)/shard_map/all_to_all | solution.py:114
  223.2 12.2 %all-to-all-start.5 = ((bf16[16,20,256]{2,1,0:T(8,128)(2,1)}), bf16[16,20,256]{2,1,0:T(8,128)(2,1)S(1)}, u32[]{:S(2)}, u32[]{:S(2)}) async-start(bf16[16,20,256]{2,1,0:T(8,128)(2,1)} %broadcast_in_dim.22), calls=%async_computation.5 | async-start | bytes 393216 | tf_op jit(solution)/shard_map/all_to_all | solution.py:67
  236.2 11.5 %all-to-all-done.5 = bf16[16,20,256]{2,1,0:T(8,128)(2,1)S(1)} async-done(((bf16[16,20,256]{2,1,0:T(8,128)(2,1)}), bf16[16,20,256]{2,1,0:T(8,128)(2,1)S(1)}, u32[]{:S(2)}, u32[]{:S(2)}) %all-to-all-start.5) | async-done | bytes 163872 | tf_op jit(solution)/shard_map/all_to_all | solution.py:67
  248.5 10.3 %all-to-all-start.6 = ((bf16[32,20,256]{2,1,0:T(8,128)(2,1)}), bf16[32,20,256]{2,1,0:T(8,128)(2,1)S(1)}, u32[]{:S(2)}, u32[]{:S(2)}) async-start(bf16[32,20,256]{2,1,0:T(8,128)(2,1)} %broadcast_in_dim.46), calls=%async_computation.6 | async-start | bytes 786432 | tf_op jit(solution)/shard_map/all_to_all | solution.py:67
  260.1 8.9 %all-to-all-done.6 = bf16[32,20,256]{2,1,0:T(8,128)(2,1)S(1)} async-done(((bf16[32,20,256]{2,1,0:T(8,128)(2,1)}), bf16[32,20,256]{2,1,0:T(8,128)(2,1)S(1)}, u32[]{:S(2)}, u32[]{:S(2)}) %all-to-all-start.6) | async-done | bytes 327712 | tf_op jit(solution)/shard_map/all_to_all | solution.py:67
  (84 shorter events, 36.1 us)
Async XLA Ops:
  3.1 13.1 %copy-start.11 = (bf16[1,160,640]{2,1,0:T(8,128)(2,1)S(1)}, bf16[1,160,640]{2,1,0:T(8,128)(2,1)}, u32[]{:S(2)}) copy-start(bf16[1,160,640]{2,1,0:T(8,128)(2,1)} %param.8) | copy-start | bytes 614404
  3.1 13.1 %copy-start.12 = (bf16[1,640,160]{1,2,0:T(8,128)(2,1)S(1)}, bf16[1,640,160]{1,2,0:T(8,128)(2,1)}, u32[]{:S(2)}) copy-start(bf16[1,640,160]{1,2,0:T(8,128)(2,1)} %param.7) | copy-start | bytes 614404
  5.8 56.7 %all-to-all-start = ((bf16[2,32,8,640]{3,2,0,1:T(8,128)(2,1)}), bf16[2,32,8,640]{3,2,0,1:T(8,128)(2,1)S(1)}, u32[]{:S(2)}, u32[]{:S(2)}) async-start(bf16[2,32,8,640]{3,2,0,1:T(8,128)(2,1)} %pad_maximum_fusion.1), calls=%async_computation | async-start | bytes 1310720 | tf_op jit(solution)/shard_map/all_to_all | solution.py:90
  16.3 46.3 %collective-permute-start = (bf16[2,160,640]{2,1,0:T(8,128)(2,1)S(1)}, bf16[2,160,640]{2,1,0:T(8,128)(2,1)S(1)}, u32[]{:S(2)}, u32[]{:S(2)}) collective-permute-start(bf16[2,160,640]{2,1,0:T(8,128)(2,1)S(1)} %pad_maximum_fusion.2), channel_id=1, source_target_pairs={{0,32},{32,64},{64,96},{96,0},{1,33},{33,65},{65,97},{97,1},{2,34}... | collective-permute-start | bytes 1228808 | tf_op jit(solution)/shard_map/ppermute | solution.py:33
  24.7 37.9 %collective-permute-start.1 = (bf16[2,160,640]{2,1,0:T(8,128)(2,1)S(1)}, bf16[2,160,640]{2,1,0:T(8,128)(2,1)S(1)}, u32[]{:S(2)}, u32[]{:S(2)}) collective-permute-start(bf16[2,160,640]{2,1,0:T(8,128)(2,1)S(1)} %pad_maximum_fusion.2), channel_id=1, source_target_pairs={{0,96},{32,0},{64,32},{96,64},{1,97},{33,1},{65,33},{97,65},{2,98}... | collective-permute-start | bytes 1228808 | tf_op jit(solution)/shard_map/ppermute | solution.py:33
  64.3 35.2 %all-to-all-start.1 = ((bf16[4,2,256,640]{3,2,1,0:T(8,128)(2,1)}), bf16[4,2,256,640]{3,2,1,0:T(8,128)(2,1)S(1)}, u32[]{:S(2)}, u32[]{:S(2)}) async-start(bf16[4,2,256,640]{3,2,1,0:T(8,128)(2,1)} %broadcast_in_dim.16), calls=%async_computation.1 | async-start | bytes 5242880 | tf_op jit(solution)/shard_map/all_to_all | solution.py:67
  68.1 10.9 %copy-start.8 = (bf16[2,160,640]{2,1,0:T(8,128)(2,1)S(1)}, bf16[2,160,640]{2,1,0:T(8,128)(2,1)}, u32[]{:S(2)}) copy-start(bf16[2,160,640]{2,1,0:T(8,128)(2,1)} %copy-done.7) | copy-start | bytes 1228804
  68.1 13.8 %copy-start.6 = (bf16[2,160,640]{2,1,0:T(8,128)(2,1)S(1)}, bf16[2,160,640]{2,1,0:T(8,128)(2,1)}, u32[]{:S(2)}) copy-start(bf16[2,160,640]{2,1,0:T(8,128)(2,1)} %copy-done.5) | copy-start | bytes 1228804
  70.2 17.1 %collective-permute-start.2 = (bf16[160,640]{1,0:T(8,128)(2,1)S(1)}, bf16[160,640]{1,0:T(8,128)(2,1)S(1)}, u32[]{:S(2)}, u32[]{:S(2)}) collective-permute-start(bf16[160,640]{1,0:T(8,128)(2,1)S(1)} %slice_bitcast_fusion.6), channel_id=1, source_target_pairs={{0,32},{32,64},{64,96},{96,0},{1,33},{33,65},{65,97},{97,1},{2,34}... | collective-permute-start | bytes 614408 | tf_op jit(solution)/shard_map/ppermute | solution.py:33
  79.0 14.8 %collective-permute-start.3 = (bf16[160,640]{1,0:T(8,128)(2,1)S(1)}, bf16[160,640]{1,0:T(8,128)(2,1)S(1)}, u32[]{:S(2)}, u32[]{:S(2)}) collective-permute-start(bf16[160,640]{1,0:T(8,128)(2,1)S(1)} %slice_bitcast_fusion.5), channel_id=1, source_target_pairs={{0,96},{32,0},{64,32},{96,64},{1,97},{33,1},{65,33},{97,65},{2,98}... | collective-permute-start | bytes 614408 | tf_op jit(solution)/shard_map/ppermute | solution.py:33
  99.8 3.8 %copy-start.1 = (bf16[4,1,256,640]{3,2,1,0:T(8,128)(2,1)}, bf16[4,1,256,640]{3,2,1,0:T(8,128)(2,1)S(1)}, u32[]{:S(2)}) copy-start(bf16[4,1,256,640]{3,2,1,0:T(8,128)(2,1)S(1)} %get-tuple-element.16) | copy-start | bytes 3932164
  141.9 22.0 %copy-start.2 = (bf16[4,1,256,640]{3,2,1,0:T(8,128)(2,1)S(1)}, bf16[4,1,256,640]{3,2,1,0:T(8,128)(2,1)}, u32[]{:S(2)}) copy-start(bf16[4,1,256,640]{3,2,1,0:T(8,128)(2,1)} %copy-done.1) | copy-start | bytes 3932164
  144.0 50.9 %all-to-all-start.3 = ((bf16[2,32,8,640]{3,2,0,1:T(8,128)(2,1)}), bf16[2,32,8,640]{3,2,0,1:T(8,128)(2,1)S(1)}, u32[]{:S(2)}, u32[]{:S(2)}) async-start(bf16[2,32,8,640]{3,2,0,1:T(8,128)(2,1)} %copy.63), calls=%async_computation.3 | async-start | bytes 1310720 | tf_op jit(solution)/shard_map/all_to_all | solution.py:106
  166.4 23.0 %copy-start.4 = (bf16[640,640]{1,0:T(8,128)(2,1)}, bf16[640,640]{1,0:T(8,128)(2,1)S(1)}, u32[]{:S(2)}) copy-start(bf16[640,640]{1,0:T(8,128)(2,1)S(1)} %convolution_convert_fusion.2) | copy-start | bytes 2457604
  166.4 28.4 %copy-start.13 = (bf16[256,640]{1,0:T(8,128)(2,1)S(1)}, bf16[256,640]{1,0:T(8,128)(2,1)}, u32[]{:S(2)}) copy-start(bf16[256,640]{1,0:T(8,128)(2,1)} %param.9) | copy-start | bytes 983044
  166.5 18.8 %collective-permute-start.4 = (bf16[2,40,640]{2,1,0:T(8,128)(2,1)S(1)}, bf16[2,40,640]{2,1,0:T(8,128)(2,1)S(1)}, u32[]{:S(2)}, u32[]{:S(2)}) collective-permute-start(bf16[2,40,640]{2,1,0:T(8,128)(2,1)S(1)} %get-tuple-element.21), channel_id=1, source_target_pairs={{0,32},{32,64},{64,96},{96,0},{1,33},{33,65},{65,97},{97,1},{2,34}... | collective-permute-start | bytes 307208 | tf_op jit(solution)/shard_map/ppermute | solution.py:33
  171.8 13.5 %collective-permute-start.6 = (bf16[2,40,640]{2,1,0:T(8,128)(2,1)S(1)}, bf16[2,40,640]{2,1,0:T(8,128)(2,1)S(1)}, u32[]{:S(2)}, u32[]{:S(2)}) collective-permute-start(bf16[2,40,640]{2,1,0:T(8,128)(2,1)S(1)} %get-tuple-element.23), channel_id=1, source_target_pairs={{0,96},{32,0},{64,32},{96,64},{1,97},{33,1},{65,33},{97,65},{2,98}... | collective-permute-start | bytes 307208 | tf_op jit(solution)/shard_map/ppermute | solution.py:33
  185.4 18.0 %collective-permute-start.5 = (bf16[4,40,640]{2,1,0:T(8,128)(2,1)S(1)}, bf16[4,40,640]{2,1,0:T(8,128)(2,1)S(1)}, u32[]{:S(2)}, u32[]{:S(2)}) collective-permute-start(bf16[4,40,640]{2,1,0:T(8,128)(2,1)S(1)} %pad_maximum_fusion.3), channel_id=1, source_target_pairs={{0,32},{32,64},{64,96},{96,0},{1,33},{33,65},{65,97},{97,1},{2,34}... | collective-permute-start | bytes 614408 | tf_op jit(solution)/shard_map/ppermute | solution.py:33
  189.5 14.0 %collective-permute-start.7 = (bf16[4,40,640]{2,1,0:T(8,128)(2,1)S(1)}, bf16[4,40,640]{2,1,0:T(8,128)(2,1)S(1)}, u32[]{:S(2)}, u32[]{:S(2)}) collective-permute-start(bf16[4,40,640]{2,1,0:T(8,128)(2,1)S(1)} %pad_maximum_fusion.4), channel_id=1, source_target_pairs={{0,96},{32,0},{64,32},{96,64},{1,97},{33,1},{65,33},{97,65},{2,98}... | collective-permute-start | bytes 614408 | tf_op jit(solution)/shard_map/ppermute | solution.py:33
  197.0 16.6 %all-to-all-start.4 = ((bf16[32,20,256]{2,1,0:T(8,128)(2,1)}), bf16[32,20,256]{2,1,0:T(8,128)(2,1)S(1)}, u32[]{:S(2)}, u32[]{:S(2)}) async-start(bf16[32,20,256]{2,1,0:T(8,128)(2,1)} %reshape.62), calls=%async_computation.4 | async-start | bytes 786432 | tf_op jit(solution)/shard_map/all_to_all | solution.py:128
  205.2 53.9 %copy-start.3 = (bf16[640,256]{1,0:T(8,128)(2,1)S(1)}, bf16[640,256]{1,0:T(8,128)(2,1)}, u32[]{:S(2)}) copy-start(bf16[640,256]{1,0:T(8,128)(2,1)} %param.6) | copy-start | bytes 983044
  213.6 8.9 %all-to-all-start.7 = ((bf16[4,40,640]{2,1,0:T(8,128)(2,1)}), bf16[4,40,640]{2,1,0:T(8,128)(2,1)S(1)}, u32[]{:S(2)}, u32[]{:S(2)}) async-start(bf16[4,40,640]{2,1,0:T(8,128)(2,1)} %fusion.17), calls=%async_computation.7 | async-start | bytes 409600 | tf_op jit(solution)/shard_map/all_to_all | solution.py:114
  223.2 24.5 %all-to-all-start.5 = ((bf16[16,20,256]{2,1,0:T(8,128)(2,1)}), bf16[16,20,256]{2,1,0:T(8,128)(2,1)S(1)}, u32[]{:S(2)}, u32[]{:S(2)}) async-start(bf16[16,20,256]{2,1,0:T(8,128)(2,1)} %broadcast_in_dim.22), calls=%async_computation.5 | async-start | bytes 393216 | tf_op jit(solution)/shard_map/all_to_all | solution.py:67
  248.5 20.4 %all-to-all-start.6 = ((bf16[32,20,256]{2,1,0:T(8,128)(2,1)}), bf16[32,20,256]{2,1,0:T(8,128)(2,1)S(1)}, u32[]{:S(2)}, u32[]{:S(2)}) async-start(bf16[32,20,256]{2,1,0:T(8,128)(2,1)} %broadcast_in_dim.46), calls=%async_computation.6 | async-start | bytes 786432 | tf_op jit(solution)/shard_map/all_to_all | solution.py:67
  (6 other events, 9.2 us)

commit v3 on v2

--- a/solution.py
+++ b/solution.py
@@ -33,15 +33,17 @@
     return lax.ppermute(values, axis, [(i, (i + step) % size) for i in range(size)])
 
 
-def gather_hidden(weights, low, high):
-    here = lax.axis_index("h")
-    up_far = shift(low[0], "h", 1)
-    down_far = shift(high[1], "h", -1)
-    far = jnp.stack([up_far, down_far])
-    full = jnp.zeros((2, 4) + weights.shape[1:], weights.dtype)
-    for block, offset in ((weights, 0), (low, 3), (high, 1), (far, 2)):
-        full = lax.dynamic_update_slice_in_dim(full, block[:, None], (here + offset) % 4, 1)
-    return full
+ROW_PAIRS = (1, 0, 3, 2)
+WEIGHT_PAIRS = (3, 2, 1, 0)
+
+
+def swap(values, pairs):
+    return lax.ppermute(values, "y", list(enumerate(pairs)))
+
+
+def place(buffer, half, offset, block):
+    index = (half, (lax.axis_index("h") + offset) % 4, 0, 0)
+    return lax.dynamic_update_slice(buffer, block[None, None], index)
 
 
 def sum_hidden(terms):
@@ -77,6 +79,7 @@
     weights = jnp.stack([up_weight[0].T, down_weight[0]])
     from_low = shift(weights, "h", 1)
     from_high = shift(weights, "h", -1)
+    partner = swap(weights, WEIGHT_PAIRS)
 
     logits = mul(patches, slot_params, ((1,), (0,)))
     dispatch = jax.nn.softmax(logits, axis=0)
@@ -87,28 +90,66 @@
     slot_grads = mul(combine_low, output_grad, ((0,), (0,))).astype(low)
 
     both = jnp.stack([slots_in, slot_grads]).reshape(2, owners, SLOT_EXP, width)
+    both, from_low, from_high, partner = lax.optimization_barrier(
+        (both, from_low, from_high, partner)
+    )
     landed = lax.all_to_all(both, OWNERS, 1, 1, tiled=True).reshape(2, slots, width)
-    landed, from_low, from_high = lax.optimization_barrier((landed, from_low, from_high))
-    full = gather_hidden(weights, from_low, from_high).reshape(2, 4 * shard, width)
-    up_rows, down_rows = full[0], full[1]
-    rows = everywhere(landed, "y", 4)
-    rows_in = rows[:, 0].reshape(4 * slots, width)
-    grads_in = rows[:, 1].reshape(4 * slots, width)
+    up_far = shift(from_low[0], "h", 1)
+    down_far = shift(from_high[1], "h", -1)
+    partner_low = swap(from_low, WEIGHT_PAIRS)
+    partner_high = swap(from_high, WEIGHT_PAIRS)
+    landed, up_far, down_far, partner_low, partner_high = lax.optimization_barrier(
+        (landed, up_far, down_far, partner_low, partner_high)
+    )
+    their_rows = swap(landed, ROW_PAIRS)
+    far = (up_far, down_far)
+    partner_far = (swap(up_far, WEIGHT_PAIRS), swap(down_far, WEIGHT_PAIRS))
 
-    hidden = mul(rows_in, up_rows, ((1,), (1,)))
-    act_grad = mul(grads_in, down_rows, ((1,), (1,)))
-    activation = gelu_value(hidden).astype(low)
-    hidden_grad = (act_grad * gelu_slope(hidden)).astype(low)
-    part_out = mul(activation, down_rows, ((1,), (0,))).astype(low)
-    part_in = mul(hidden_grad, up_rows, ((1,), (0,))).astype(low)
-    parts = jnp.stack([part_out.reshape(4, slots, width), part_in.reshape(4, slots, width)], axis=1)
-    summed = jnp.sum(lax.all_to_all(parts, "y", 0, 0).astype(jnp.float32), axis=0).astype(low)
+    def assemble(which):
+        buffer = jnp.zeros((2, 4, shard, width), low)
+        for half, blocks in enumerate(
+            (
+                (weights[which], from_high[which], far[which], from_low[which]),
+                (partner[which], partner_high[which], partner_far[which], partner_low[which]),
+            )
+        ):
+            for offset, block in enumerate(blocks):
+                buffer = place(buffer, half, offset, block)
+        return buffer.reshape(8 * shard, width)
+
+    up_rows, down_rows = assemble(0), assemble(1)
+
+    def expert(rows_in, grads_in):
+        hidden = mul(rows_in, up_rows, ((1,), (1,)))
+        act_grad = mul(grads_in, down_rows, ((1,), (1,)))
+        activation = gelu_value(hidden).astype(low)
+        hidden_grad = (act_grad * gelu_slope(hidden)).astype(low)
+        part_out = mul(activation, down_rows, ((1,), (0,)))
+        part_in = mul(hidden_grad, up_rows, ((1,), (0,)))
+        return hidden_grad, part_out, part_in
+
+    their_hidden, their_out, their_in = expert(their_rows[0], their_rows[1])
+    out_back = swap(their_out.astype(low), ROW_PAIRS)
+    in_back = swap(their_in.astype(low), ROW_PAIRS)
+    own_hidden, own_out, own_in = expert(landed[0], landed[1])
+    summed = jnp.stack(
+        [
+            (own_out + out_back.astype(jnp.float32)).astype(low),
+            (own_in + in_back.astype(jnp.float32)).astype(low),
+        ]
+    )
     back = lax.all_to_all(
         summed.reshape(2, owners, SLOT_EXP, width), OWNERS, 1, 1, tiled=True
     ).reshape(2, slots, width)
     slot_out, slot_in_grad = back[0], back[1]
 
-    up_term = mul(rows_in, hidden_grad, ((0,), (0,))).astype(low)
+    def up_half(half):
+        columns = slice(half * 4 * shard, (half + 1) * 4 * shard)
+        term = mul(landed[0], own_hidden[:, columns], ((0,), (0,)))
+        return term + mul(their_rows[0], their_hidden[:, columns], ((0,), (0,)))
+
+    up_other = swap(up_half(1).astype(low), WEIGHT_PAIRS)
+    up_term = (up_half(0) + up_other.astype(jnp.float32)).astype(low)
     up_term = up_term.reshape(4, 4, width // 16, 4 * shard)
     up_sum = sum_hidden(up_term)
     up_grad = lax.all_to_all(up_sum, "y", 0, 0)

time: 271 us -> 285 us (1.052)
  blocking collectives: 32.8 us -> 0 us
  starting transfers between devices: 108 us -> 125 us
  waiting for transfers between devices: 94.7 us -> 110 us
  local copies, waits for them, and re-layouts: 12.8 us -> 21.7 us
  matrix products: 14.4 us -> 19.4 us
    all_to_all x1, waiting for transfers between devices: 34.9 us -> 0.01 us  [local(): lax.all_to_all(both, OWNERS, 1, 1, tiled=True).reshape(2, slots, width)]
    all_to_all x1 -> x0, blocking collectives: 32.8 us -> none  [local(): lax.all_to_all(parts, 'y', 0, 0).astype(jnp.float32)]
    ppermute x8, waiting for transfers between devices: 21.2 us -> 51.5 us  [shift(): lax.ppermute(values, axis, [(i, (i + step) % size) for i in range(size)])]
    ppermute x0 -> x9, starting transfers between devices: none -> 29.5 us  [swap(): return lax.ppermute(values, 'y', list(enumerate(pairs)))]
    ppermute x0 -> x9, waiting for transfers between devices: none -> 23.7 us  [swap(): return lax.ppermute(values, 'y', list(enumerate(pairs)))]
    dynamic_update_slice x2 -> x10, local copies, waits for them, and re-layouts: 0.11 us -> 10.9 us  [place(): return lax.dynamic_update_slice(buffer, block[None, None], index)]
    all_to_all x3 -> x2, starting transfers between devices: 26.1 us -> 15.5 us  [everywhere(): return lax.all_to_all(spread, axes, 0, 0)]
    all_to_all x1, starting transfers between devices: 6.46 us -> 15.4 us  [local(): lax.all_to_all(piece, ('y', 'x', 'c'), 0, 0).astype(jnp.float32)]
  transfers between devices with their start and end apart: 15 -> 23, of which waited for: 9 -> 12; matrix products, arithmetic and copies ran while one was open for 5% -> 13% of each run, Pallas kernels for 0% -> 0%
where the time goes in v3:
time: 285 us; the launch traced here: 284 us
  starting transfers between devices  125 us (44%)
  waiting for transfers between devices  110 us (39%)
  local copies, waits for them, and re-layouts  21.7 us (8%)
  matrix products  19.4 us (7%)
  other arithmetic  6.41 us (2%)
    ppermute x8, waiting for transfers between devices, shift(): lax.ppermute(values, axis, [(i, (i + step) % size) for i in range(size)])  51.5 us
    ppermute x8, starting transfers between devices, shift(): lax.ppermute(values, axis, [(i, (i + step) % size) for i in range(size)])  44.6 us
    ppermute x9, starting transfers between devices, swap(): return lax.ppermute(values, 'y', list(enumerate(pairs)))  29.5 us
    ppermute x9, waiting for transfers between devices, swap(): return lax.ppermute(values, 'y', list(enumerate(pairs)))  23.7 us
    all_to_all x2, waiting for transfers between devices, everywhere(): return lax.all_to_all(spread, axes, 0, 0)  20.3 us
    dot_general x20, matrix products, mul(): lax.dot_general(a, b, (dims, ((), ())), preferred_element_type=jnp.float32)  19.4 us
    all_to_all x2, starting transfers between devices, everywhere(): return lax.all_to_all(spread, axes, 0, 0)  15.5 us
    all_to_all x1, starting transfers between devices, local(): lax.all_to_all(piece, ('y', 'x', 'c'), 0, 0).astype(jnp.float32)  15.4 us
  transfers between devices with their start and end apart: 23, of which 12 were waited for; matrix products, arithmetic and copies ran while one was open for 13% of the time, Pallas kernels for 0%

profile of v3, /device:TPU:1, one launch (start us, length us, event | category | flops | bytes accessed | tf_op | source)
XLA Modules:
  0.0 283.9 jit_solution(16254524225815919388)
XLA Ops:
  1.8 9.6 %collective-permute-start = (bf16[2,160,640]{2,1,0:T(8,128)(2,1)S(1)}, bf16[2,160,640]{2,1,0:T(8,128)(2,1)}, u32[]{:S(2)}, u32[]{:S(2)}) collective-permute-start(bf16[2,160,640]{2,1,0:T(8,128)(2,1)S(1)} %pad_maximum_fusion.2), channel_id=1, source_target_pairs={{0,32},{32,64},{64,96},{96,0},{1,33},{33,65},{65,97},{97,1},{2,34}... | collective-permute-start | bytes 1228808 | tf_op jit(solution)/shard_map/ppermute | solution.py:33
  11.5 5.6 %collective-permute-start.1 = (bf16[2,160,640]{2,1,0:T(8,128)(2,1)S(1)}, bf16[2,160,640]{2,1,0:T(8,128)(2,1)}, u32[]{:S(2)}, u32[]{:S(2)}) collective-permute-start(bf16[2,160,640]{2,1,0:T(8,128)(2,1)S(1)} %pad_maximum_fusion.2), channel_id=1, source_target_pairs={{0,96},{32,0},{64,32},{96,64},{1,97},{33,1},{65,33},{97,65},{2,98}... | collective-permute-start | bytes 1228808 | tf_op jit(solution)/shard_map/ppermute | solution.py:33
  17.0 4.6 %collective-permute-start.2 = (bf16[2,160,640]{2,1,0:T(8,128)(2,1)S(1)}, bf16[2,160,640]{2,1,0:T(8,128)(2,1)S(1)}, u32[]{:S(2)}, u32[]{:S(2)}) collective-permute-start(bf16[2,160,640]{2,1,0:T(8,128)(2,1)S(1)} %pad_maximum_fusion.2), channel_id=1, source_target_pairs={{0,384},{128,256},{256,128},{384,0},{1,385},{129,257},{257,129},{3... | collective-permute-start | bytes 1228808 | tf_op jit(solution)/shard_map/ppermute | solution.py:41
  28.6 27.6 %collective-permute-done.1 = bf16[2,160,640]{2,1,0:T(8,128)(2,1)} collective-permute-done((bf16[2,160,640]{2,1,0:T(8,128)(2,1)S(1)}, bf16[2,160,640]{2,1,0:T(8,128)(2,1)}, u32[]{:S(2)}, u32[]{:S(2)}) %collective-permute-start.1) | collective-permute-done | bytes 409632 | tf_op jit(solution)/shard_map/ppermute | solution.py:33
  57.0 5.4 %all-to-all-start = ((bf16[2,32,8,640]{3,2,0,1:T(8,128)(2,1)}), bf16[2,32,8,640]{3,2,0,1:T(8,128)(2,1)S(1)}, u32[]{:S(2)}, u32[]{:S(2)}) async-start(bf16[2,32,8,640]{3,2,0,1:T(8,128)(2,1)} %pad_maximum_fusion), calls=%async_computation | async-start | bytes 1310720 | tf_op jit(solution)/shard_map/all_to_all | solution.py:96
  64.7 4.6 %collective-permute-start.5 = (bf16[2,160,640]{2,1,0:T(8,128)(2,1)}, bf16[2,160,640]{2,1,0:T(8,128)(2,1)}, u32[]{:S(2)}, u32[]{:S(2)}) collective-permute-start(bf16[2,160,640]{2,1,0:T(8,128)(2,1)} %collective-permute-done), channel_id=1, source_target_pairs={{0,384},{128,256},{256,128},{384,0},{1,385},{129,257},{257,129},{3... | collective-permute-start | bytes 1228808 | tf_op jit(solution)/shard_map/ppermute | solution.py:41
  71.0 9.0 %collective-permute-start.3 = (bf16[160,640]{1,0:T(8,128)(2,1)}, bf16[160,640]{1,0:T(8,128)(2,1)}, u32[]{:S(2)}, u32[]{:S(2)}) collective-permute-start(bf16[160,640]{1,0:T(8,128)(2,1)} %slice_bitcast_fusion.12), channel_id=1, source_target_pairs={{0,32},{32,64},{64,96},{96,0},{1,33},{33,65},{65,97},{97,1},{2,34}... | collective-permute-start | bytes 614408 | tf_op jit(solution)/shard_map/ppermute | solution.py:33
  87.3 9.8 %collective-permute-done.3 = bf16[160,640]{1,0:T(8,128)(2,1)} collective-permute-done((bf16[160,640]{1,0:T(8,128)(2,1)}, bf16[160,640]{1,0:T(8,128)(2,1)}, u32[]{:S(2)}, u32[]{:S(2)}) %collective-permute-start.3) | collective-permute-done | bytes 204832 | tf_op jit(solution)/shard_map/ppermute | solution.py:33
  97.1 6.2 %collective-permute-done.4 = bf16[160,640]{1,0:T(8,128)(2,1)} collective-permute-done((bf16[160,640]{1,0:T(8,128)(2,1)}, bf16[160,640]{1,0:T(8,128)(2,1)}, u32[]{:S(2)}, u32[]{:S(2)}) %collective-permute-start.4) | collective-permute-done | bytes 204832 | tf_op jit(solution)/shard_map/ppermute | solution.py:33
  103.4 4.5 %collective-permute-start.7 = (bf16[160,640]{1,0:T(8,128)(2,1)}, bf16[160,640]{1,0:T(8,128)(2,1)S(1)}, u32[]{:S(2)}, u32[]{:S(2)}) collective-permute-start(bf16[160,640]{1,0:T(8,128)(2,1)} %collective-permute-done.3), channel_id=1, source_target_pairs={{0,384},{128,256},{256,128},{384,0},{1,385},{129,257},{257,129},{3... | collective-permute-start | bytes 614408 | tf_op jit(solution)/shard_map/ppermute | solution.py:41
  137.2 7.5 %collective-permute-done.11 = bf16[256,640]{1,0:T(8,128)(2,1)S(1)} collective-permute-done((bf16[256,640]{1,0:T(8,128)(2,1)S(1)}, bf16[256,640]{1,0:T(8,128)(2,1)S(1)}, u32[]{:S(2)}, u32[]{:S(2)}) %collective-permute-start.11) | collective-permute-done | bytes 327712 | tf_op jit(solution)/shard_map/ppermute | solution.py:41
  146.3 11.2 %all-to-all-start.1 = ((bf16[2,32,8,640]{3,2,0,1:T(8,128)(2,1)}), bf16[2,32,8,640]{3,2,0,1:T(8,128)(2,1)S(1)}, u32[]{:S(2)}, u32[]{:S(2)}) async-start(bf16[2,32,8,640]{3,2,0,1:T(8,128)(2,1)} %pad_maximum_fusion.1), calls=%async_computation.1 | async-start | bytes 1310720 | tf_op jit(solution)/shard_map/all_to_all | solution.py:141
  159.1 4.6 %collective-permute-start.12 = (bf16[640,640]{1,0:T(8,128)(2,1)S(1)}, bf16[640,640]{1,0:T(8,128)(2,1)}, u32[]{:S(2)}, u32[]{:S(2)}) collective-permute-start(bf16[640,640]{1,0:T(8,128)(2,1)S(1)} %add_convert_fusion.1), channel_id=1, source_target_pairs={{0,384},{128,256},{256,128},{384,0},{1,385},{129,257},{257,129},{3... | collective-permute-start | bytes 2457608 | tf_op jit(solution)/shard_map/ppermute | solution.py:41
  165.7 16.2 %collective-permute-done.12 = bf16[640,640]{1,0:T(8,128)(2,1)} collective-permute-done((bf16[640,640]{1,0:T(8,128)(2,1)S(1)}, bf16[640,640]{1,0:T(8,128)(2,1)}, u32[]{:S(2)}, u32[]{:S(2)}) %collective-permute-start.12) | collective-permute-done | bytes 819232 | tf_op jit(solution)/shard_map/ppermute | solution.py:41
  183.4 4.0 %collective-permute-start.13 = (bf16[2,40,640]{2,1,0:T(8,128)(2,1)S(1)}, bf16[2,40,640]{2,1,0:T(8,128)(2,1)S(1)}, u32[]{:S(2)}, u32[]{:S(2)}) collective-permute-start(bf16[2,40,640]{2,1,0:T(8,128)(2,1)S(1)} %get-tuple-element.29), channel_id=1, source_target_pairs={{0,32},{32,64},{64,96},{96,0},{1,33},{33,65},{65,97},{97,1},{2,34}... | collective-permute-start | bytes 307208 | tf_op jit(solution)/shard_map/ppermute | solution.py:33
  187.4 5.3 %collective-permute-start.15 = (bf16[2,40,640]{2,1,0:T(8,128)(2,1)S(1)}, bf16[2,40,640]{2,1,0:T(8,128)(2,1)S(1)}, u32[]{:S(2)}, u32[]{:S(2)}) collective-permute-start(bf16[2,40,640]{2,1,0:T(8,128)(2,1)S(1)} %get-tuple-element.31), channel_id=1, source_target_pairs={{0,96},{32,0},{64,32},{96,64},{1,97},{33,1},{65,33},{97,65},{2,98}... | collective-permute-start | bytes 307208 | tf_op jit(solution)/shard_map/ppermute | solution.py:33
  197.0 6.3 %collective-permute-start.16 = (bf16[4,40,640]{2,1,0:T(8,128)(2,1)S(1)}, bf16[4,40,640]{2,1,0:T(8,128)(2,1)S(1)}, u32[]{:S(2)}, u32[]{:S(2)}) collective-permute-start(bf16[4,40,640]{2,1,0:T(8,128)(2,1)S(1)} %pad_maximum_fusion.4), channel_id=1, source_target_pairs={{0,96},{32,0},{64,32},{96,64},{1,97},{33,1},{65,33},{97,65},{2,98}... | collective-permute-start | bytes 614408 | tf_op jit(solution)/shard_map/ppermute | solution.py:33
  209.2 15.4 %all-to-all-start.2 = ((bf16[32,20,256]{2,1,0:T(8,128)(2,1)}), bf16[32,20,256]{2,1,0:T(8,128)(2,1)S(1)}, u32[]{:S(2)}, u32[]{:S(2)}) async-start(bf16[32,20,256]{2,1,0:T(8,128)(2,1)} %reshape.65), calls=%async_computation.2 | async-start | bytes 786432 | tf_op jit(solution)/shard_map/all_to_all | solution.py:169
  225.5 9.4 %all-to-all-done.2 = bf16[32,20,256]{2,1,0:T(8,128)(2,1)S(1)} async-done(((bf16[32,20,256]{2,1,0:T(8,128)(2,1)}), bf16[32,20,256]{2,1,0:T(8,128)(2,1)S(1)}, u32[]{:S(2)}, u32[]{:S(2)}) %all-to-all-start.2) | async-done | bytes 327712 | tf_op jit(solution)/shard_map/all_to_all | solution.py:169
  238.3 5.1 %all-to-all-done.5 = bf16[4,40,640]{2,1,0:T(8,128)(2,1)S(1)} async-done(((bf16[4,40,640]{2,1,0:T(8,128)(2,1)}), bf16[4,40,640]{2,1,0:T(8,128)(2,1)S(1)}, u32[]{:S(2)}, u32[]{:S(2)}) %all-to-all-start.5) | async-done | bytes 204832 | tf_op jit(solution)/shard_map/all_to_all | solution.py:155
  244.1 5.6 %all-to-all-start.3 = ((bf16[16,20,256]{2,1,0:T(8,128)(2,1)}), bf16[16,20,256]{2,1,0:T(8,128)(2,1)S(1)}, u32[]{:S(2)}, u32[]{:S(2)}) async-start(bf16[16,20,256]{2,1,0:T(8,128)(2,1)} %broadcast_in_dim.16), calls=%async_computation.3 | async-start | bytes 393216 | tf_op jit(solution)/shard_map/all_to_all | solution.py:69
  250.6 11.5 %all-to-all-done.3 = bf16[16,20,256]{2,1,0:T(8,128)(2,1)S(1)} async-done(((bf16[16,20,256]{2,1,0:T(8,128)(2,1)}), bf16[16,20,256]{2,1,0:T(8,128)(2,1)S(1)}, u32[]{:S(2)}, u32[]{:S(2)}) %all-to-all-start.3) | async-done | bytes 163872 | tf_op jit(solution)/shard_map/all_to_all | solution.py:69
  262.9 10.0 %all-to-all-start.4 = ((bf16[32,20,256]{2,1,0:T(8,128)(2,1)}), bf16[32,20,256]{2,1,0:T(8,128)(2,1)S(1)}, u32[]{:S(2)}, u32[]{:S(2)}) async-start(bf16[32,20,256]{2,1,0:T(8,128)(2,1)} %broadcast_in_dim.17), calls=%async_computation.4 | async-start | bytes 786432 | tf_op jit(solution)/shard_map/all_to_all | solution.py:69
  274.2 8.9 %all-to-all-done.4 = bf16[32,20,256]{2,1,0:T(8,128)(2,1)S(1)} async-done(((bf16[32,20,256]{2,1,0:T(8,128)(2,1)}), bf16[32,20,256]{2,1,0:T(8,128)(2,1)S(1)}, u32[]{:S(2)}, u32[]{:S(2)}) %all-to-all-start.4) | async-done | bytes 327712 | tf_op jit(solution)/shard_map/all_to_all | solution.py:69
  (109 shorter events, 74.6 us)
Async XLA Ops:
  1.8 26.8 %collective-permute-start = (bf16[2,160,640]{2,1,0:T(8,128)(2,1)S(1)}, bf16[2,160,640]{2,1,0:T(8,128)(2,1)}, u32[]{:S(2)}, u32[]{:S(2)}) collective-permute-start(bf16[2,160,640]{2,1,0:T(8,128)(2,1)S(1)} %pad_maximum_fusion.2), channel_id=1, source_target_pairs={{0,32},{32,64},{64,96},{96,0},{1,33},{33,65},{65,97},{97,1},{2,34}... | collective-permute-start | bytes 1228808 | tf_op jit(solution)/shard_map/ppermute | solution.py:33
  11.5 44.8 %collective-permute-start.1 = (bf16[2,160,640]{2,1,0:T(8,128)(2,1)S(1)}, bf16[2,160,640]{2,1,0:T(8,128)(2,1)}, u32[]{:S(2)}, u32[]{:S(2)}) collective-permute-start(bf16[2,160,640]{2,1,0:T(8,128)(2,1)S(1)} %pad_maximum_fusion.2), channel_id=1, source_target_pairs={{0,96},{32,0},{64,32},{96,64},{1,97},{33,1},{65,33},{97,65},{2,98}... | collective-permute-start | bytes 1228808 | tf_op jit(solution)/shard_map/ppermute | solution.py:33
  17.0 39.2 %collective-permute-start.2 = (bf16[2,160,640]{2,1,0:T(8,128)(2,1)S(1)}, bf16[2,160,640]{2,1,0:T(8,128)(2,1)S(1)}, u32[]{:S(2)}, u32[]{:S(2)}) collective-permute-start(bf16[2,160,640]{2,1,0:T(8,128)(2,1)S(1)} %pad_maximum_fusion.2), channel_id=1, source_target_pairs={{0,384},{128,256},{256,128},{384,0},{1,385},{129,257},{257,129},{3... | collective-permute-start | bytes 1228808 | tf_op jit(solution)/shard_map/ppermute | solution.py:41
  24.9 37.8 %copy-start.4 = (bf16[1,640,160]{1,2,0:T(8,128)(2,1)S(1)}, bf16[1,640,160]{1,2,0:T(8,128)(2,1)}, u32[]{:S(2)}) copy-start(bf16[1,640,160]{1,2,0:T(8,128)(2,1)} %param.7) | copy-start | bytes 614404
  57.0 30.2 %all-to-all-start = ((bf16[2,32,8,640]{3,2,0,1:T(8,128)(2,1)}), bf16[2,32,8,640]{3,2,0,1:T(8,128)(2,1)S(1)}, u32[]{:S(2)}, u32[]{:S(2)}) async-start(bf16[2,32,8,640]{3,2,0,1:T(8,128)(2,1)} %pad_maximum_fusion), calls=%async_computation | async-start | bytes 1310720 | tf_op jit(solution)/shard_map/all_to_all | solution.py:96
  64.7 38.6 %collective-permute-start.5 = (bf16[2,160,640]{2,1,0:T(8,128)(2,1)}, bf16[2,160,640]{2,1,0:T(8,128)(2,1)}, u32[]{:S(2)}, u32[]{:S(2)}) collective-permute-start(bf16[2,160,640]{2,1,0:T(8,128)(2,1)} %collective-permute-done), channel_id=1, source_target_pairs={{0,384},{128,256},{256,128},{384,0},{1,385},{129,257},{257,129},{3... | collective-permute-start | bytes 1228808 | tf_op jit(solution)/shard_map/ppermute | solution.py:41
  71.0 26.1 %collective-permute-start.3 = (bf16[160,640]{1,0:T(8,128)(2,1)}, bf16[160,640]{1,0:T(8,128)(2,1)}, u32[]{:S(2)}, u32[]{:S(2)}) collective-permute-start(bf16[160,640]{1,0:T(8,128)(2,1)} %slice_bitcast_fusion.12), channel_id=1, source_target_pairs={{0,32},{32,64},{64,96},{96,0},{1,33},{33,65},{65,97},{97,1},{2,34}... | collective-permute-start | bytes 614408 | tf_op jit(solution)/shard_map/ppermute | solution.py:33
  80.0 23.4 %collective-permute-start.6 = (bf16[2,160,640]{2,1,0:T(8,128)(2,1)}, bf16[2,160,640]{2,1,0:T(8,128)(2,1)}, u32[]{:S(2)}, u32[]{:S(2)}) collective-permute-start(bf16[2,160,640]{2,1,0:T(8,128)(2,1)} %collective-permute-done.1), channel_id=1, source_target_pairs={{0,384},{128,256},{256,128},{384,0},{1,385},{129,257},{257,129},{3... | collective-permute-start | bytes 1228808 | tf_op jit(solution)/shard_map/ppermute | solution.py:41
  83.6 19.8 %collective-permute-start.4 = (bf16[160,640]{1,0:T(8,128)(2,1)}, bf16[160,640]{1,0:T(8,128)(2,1)}, u32[]{:S(2)}, u32[]{:S(2)}) collective-permute-start(bf16[160,640]{1,0:T(8,128)(2,1)} %slice_bitcast_fusion.11), channel_id=1, source_target_pairs={{0,96},{32,0},{64,32},{96,64},{1,97},{33,1},{65,33},{97,65},{2,98}... | collective-permute-start | bytes 614408 | tf_op jit(solution)/shard_map/ppermute | solution.py:33
  103.4 14.4 %collective-permute-start.7 = (bf16[160,640]{1,0:T(8,128)(2,1)}, bf16[160,640]{1,0:T(8,128)(2,1)S(1)}, u32[]{:S(2)}, u32[]{:S(2)}) collective-permute-start(bf16[160,640]{1,0:T(8,128)(2,1)} %collective-permute-done.3), channel_id=1, source_target_pairs={{0,384},{128,256},{256,128},{384,0},{1,385},{129,257},{257,129},{3... | collective-permute-start | bytes 614408 | tf_op jit(solution)/shard_map/ppermute | solution.py:41
  107.9 9.9 %collective-permute-start.8 = (bf16[160,640]{1,0:T(8,128)(2,1)}, bf16[160,640]{1,0:T(8,128)(2,1)S(1)}, u32[]{:S(2)}, u32[]{:S(2)}) collective-permute-start(bf16[160,640]{1,0:T(8,128)(2,1)} %collective-permute-done.4), channel_id=1, source_target_pairs={{0,384},{128,256},{256,128},{384,0},{1,385},{129,257},{257,129},{3... | collective-permute-start | bytes 614408 | tf_op jit(solution)/shard_map/ppermute | solution.py:41
  109.9 13.6 %collective-permute-start.9 = (bf16[2,256,640]{2,1,0:T(8,128)(2,1)S(1)}, bf16[2,256,640]{2,1,0:T(8,128)(2,1)S(1)}, u32[]{:S(2)}, u32[]{:S(2)}) collective-permute-start(bf16[2,256,640]{2,1,0:T(8,128)(2,1)S(1)} %bitcast.157), channel_id=1, source_target_pairs={{0,128},{128,0},{256,384},{384,256},{1,129},{129,1},{257,385},{385... | collective-permute-start | bytes 1966088 | tf_op jit(solution)/shard_map/ppermute | solution.py:41
  126.5 8.5 %collective-permute-start.10 = (bf16[256,640]{1,0:T(8,128)(2,1)S(1)}, bf16[256,640]{1,0:T(8,128)(2,1)S(1)}, u32[]{:S(2)}, u32[]{:S(2)}) collective-permute-start(bf16[256,640]{1,0:T(8,128)(2,1)S(1)} %convolution_convert_fusion.2), channel_id=1, source_target_pairs={{0,128},{128,0},{256,384},{384,256},{1,129},{129,1},{257,385},{385... | collective-permute-start | bytes 983048 | tf_op jit(solution)/shard_map/ppermute | solution.py:41
  133.0 11.6 %collective-permute-start.11 = (bf16[256,640]{1,0:T(8,128)(2,1)S(1)}, bf16[256,640]{1,0:T(8,128)(2,1)S(1)}, u32[]{:S(2)}, u32[]{:S(2)}) collective-permute-start(bf16[256,640]{1,0:T(8,128)(2,1)S(1)} %convolution_convert_fusion.1), channel_id=1, source_target_pairs={{0,128},{128,0},{256,384},{384,256},{1,129},{129,1},{257,385},{385... | collective-permute-start | bytes 983048 | tf_op jit(solution)/shard_map/ppermute | solution.py:41
  146.3 60.6 %all-to-all-start.1 = ((bf16[2,32,8,640]{3,2,0,1:T(8,128)(2,1)}), bf16[2,32,8,640]{3,2,0,1:T(8,128)(2,1)S(1)}, u32[]{:S(2)}, u32[]{:S(2)}) async-start(bf16[2,32,8,640]{3,2,0,1:T(8,128)(2,1)} %pad_maximum_fusion.1), calls=%async_computation.1 | async-start | bytes 1310720 | tf_op jit(solution)/shard_map/all_to_all | solution.py:141
  159.1 22.8 %collective-permute-start.12 = (bf16[640,640]{1,0:T(8,128)(2,1)S(1)}, bf16[640,640]{1,0:T(8,128)(2,1)}, u32[]{:S(2)}, u32[]{:S(2)}) collective-permute-start(bf16[640,640]{1,0:T(8,128)(2,1)S(1)} %add_convert_fusion.1), channel_id=1, source_target_pairs={{0,384},{128,256},{256,128},{384,0},{1,385},{129,257},{257,129},{3... | collective-permute-start | bytes 2457608 | tf_op jit(solution)/shard_map/ppermute | solution.py:41
  183.4 9.7 %collective-permute-start.13 = (bf16[2,40,640]{2,1,0:T(8,128)(2,1)S(1)}, bf16[2,40,640]{2,1,0:T(8,128)(2,1)S(1)}, u32[]{:S(2)}, u32[]{:S(2)}) collective-permute-start(bf16[2,40,640]{2,1,0:T(8,128)(2,1)S(1)} %get-tuple-element.29), channel_id=1, source_target_pairs={{0,32},{32,64},{64,96},{96,0},{1,33},{33,65},{65,97},{97,1},{2,34}... | collective-permute-start | bytes 307208 | tf_op jit(solution)/shard_map/ppermute | solution.py:33
  187.4 9.5 %collective-permute-start.15 = (bf16[2,40,640]{2,1,0:T(8,128)(2,1)S(1)}, bf16[2,40,640]{2,1,0:T(8,128)(2,1)S(1)}, u32[]{:S(2)}, u32[]{:S(2)}) collective-permute-start(bf16[2,40,640]{2,1,0:T(8,128)(2,1)S(1)} %get-tuple-element.31), channel_id=1, source_target_pairs={{0,96},{32,0},{64,32},{96,64},{1,97},{33,1},{65,33},{97,65},{2,98}... | collective-permute-start | bytes 307208 | tf_op jit(solution)/shard_map/ppermute | solution.py:33
  197.0 27.7 %collective-permute-start.16 = (bf16[4,40,640]{2,1,0:T(8,128)(2,1)S(1)}, bf16[4,40,640]{2,1,0:T(8,128)(2,1)S(1)}, u32[]{:S(2)}, u32[]{:S(2)}) collective-permute-start(bf16[4,40,640]{2,1,0:T(8,128)(2,1)S(1)} %pad_maximum_fusion.4), channel_id=1, source_target_pairs={{0,96},{32,0},{64,32},{96,64},{1,97},{33,1},{65,33},{97,65},{2,98}... | collective-permute-start | bytes 614408 | tf_op jit(solution)/shard_map/ppermute | solution.py:33
  204.0 20.6 %collective-permute-start.14 = (bf16[4,40,640]{2,1,0:T(8,128)(2,1)}, bf16[4,40,640]{2,1,0:T(8,128)(2,1)S(1)}, u32[]{:S(2)}, u32[]{:S(2)}) collective-permute-start(bf16[4,40,640]{2,1,0:T(8,128)(2,1)} %pad_maximum_fusion.3), channel_id=1, source_target_pairs={{0,32},{32,64},{64,96},{96,0},{1,33},{33,65},{65,97},{97,1},{2,34}... | collective-permute-start | bytes 614408 | tf_op jit(solution)/shard_map/ppermute | solution.py:33
  209.2 25.6 %all-to-all-start.2 = ((bf16[32,20,256]{2,1,0:T(8,128)(2,1)}), bf16[32,20,256]{2,1,0:T(8,128)(2,1)S(1)}, u32[]{:S(2)}, u32[]{:S(2)}) async-start(bf16[32,20,256]{2,1,0:T(8,128)(2,1)} %reshape.65), calls=%async_computation.2 | async-start | bytes 786432 | tf_op jit(solution)/shard_map/all_to_all | solution.py:169
  234.8 8.6 %all-to-all-start.5 = ((bf16[4,40,640]{2,1,0:T(8,128)(2,1)}), bf16[4,40,640]{2,1,0:T(8,128)(2,1)S(1)}, u32[]{:S(2)}, u32[]{:S(2)}) async-start(bf16[4,40,640]{2,1,0:T(8,128)(2,1)} %fusion.29), calls=%async_computation.5 | async-start | bytes 409600 | tf_op jit(solution)/shard_map/all_to_all | solution.py:155
  244.1 17.9 %all-to-all-start.3 = ((bf16[16,20,256]{2,1,0:T(8,128)(2,1)}), bf16[16,20,256]{2,1,0:T(8,128)(2,1)S(1)}, u32[]{:S(2)}, u32[]{:S(2)}) async-start(bf16[16,20,256]{2,1,0:T(8,128)(2,1)} %broadcast_in_dim.16), calls=%async_computation.3 | async-start | bytes 393216 | tf_op jit(solution)/shard_map/all_to_all | solution.py:69
  262.9 20.2 %all-to-all-start.4 = ((bf16[32,20,256]{2,1,0:T(8,128)(2,1)}), bf16[32,20,256]{2,1,0:T(8,128)(2,1)S(1)}, u32[]{:S(2)}, u32[]{:S(2)}) async-start(bf16[32,20,256]{2,1,0:T(8,128)(2,1)} %broadcast_in_dim.17), calls=%async_computation.4 | async-start | bytes 786432 | tf_op jit(solution)/shard_map/all_to_all | solution.py:69
  (14 other events, 197.5 us)

commit v4 on v2

--- a/solution.py
+++ b/solution.py
@@ -33,17 +33,6 @@
     return lax.ppermute(values, axis, [(i, (i + step) % size) for i in range(size)])
 
 
-def gather_hidden(weights, low, high):
-    here = lax.axis_index("h")
-    up_far = shift(low[0], "h", 1)
-    down_far = shift(high[1], "h", -1)
-    far = jnp.stack([up_far, down_far])
-    full = jnp.zeros((2, 4) + weights.shape[1:], weights.dtype)
-    for block, offset in ((weights, 0), (low, 3), (high, 1), (far, 2)):
-        full = lax.dynamic_update_slice_in_dim(full, block[:, None], (here + offset) % 4, 1)
-    return full
-
-
 def sum_hidden(terms):
     here = lax.axis_index("h")
 
@@ -62,6 +51,17 @@
     return total.astype(terms.dtype)
 
 
+def spread_rows(terms):
+    here = lax.axis_index("y")
+    result = jnp.zeros(terms.shape, terms.dtype)
+    for step in range(4):
+        block = lax.dynamic_index_in_dim(terms, (here + step) % 4, 0, keepdims=True)
+        if step:
+            block = shift(block, "y", step)
+        result = lax.dynamic_update_slice_in_dim(result, block, (here - step) % 4, 0)
+    return jnp.transpose(result, (1, 0, 2))
+
+
 def everywhere(values, axes, count):
     spread = jnp.broadcast_to(values[None], (count,) + values.shape)
     return lax.all_to_all(spread, axes, 0, 0)
@@ -74,10 +74,6 @@
     shard = up_weight.shape[2]
     low = jnp.bfloat16
 
-    weights = jnp.stack([up_weight[0].T, down_weight[0]])
-    from_low = shift(weights, "h", 1)
-    from_high = shift(weights, "h", -1)
-
     logits = mul(patches, slot_params, ((1,), (0,)))
     dispatch = jax.nn.softmax(logits, axis=0)
     combine = jax.nn.softmax(logits, axis=1)
@@ -88,9 +84,9 @@
 
     both = jnp.stack([slots_in, slot_grads]).reshape(2, owners, SLOT_EXP, width)
     landed = lax.all_to_all(both, OWNERS, 1, 1, tiled=True).reshape(2, slots, width)
-    landed, from_low, from_high = lax.optimization_barrier((landed, from_low, from_high))
-    full = gather_hidden(weights, from_low, from_high).reshape(2, 4 * shard, width)
-    up_rows, down_rows = full[0], full[1]
+    up_rows = lax.all_gather(up_weight[0].T, "h").reshape(4 * shard, width)
+    landed, up_rows, down_rows = lax.optimization_barrier((landed, up_rows, down_weight[0]))
+    down_rows = lax.all_gather(down_rows, "h").reshape(4 * shard, width)
     rows = everywhere(landed, "y", 4)
     rows_in = rows[:, 0].reshape(4 * slots, width)
     grads_in = rows[:, 1].reshape(4 * slots, width)
@@ -103,16 +99,16 @@
     part_in = mul(hidden_grad, up_rows, ((1,), (0,))).astype(low)
     parts = jnp.stack([part_out.reshape(4, slots, width), part_in.reshape(4, slots, width)], axis=1)
     summed = jnp.sum(lax.all_to_all(parts, "y", 0, 0).astype(jnp.float32), axis=0).astype(low)
+    up_term = mul(rows_in, hidden_grad, ((0,), (0,))).astype(low)
+    up_sum = sum_hidden(up_term.reshape(4, 4, width // 16, 4 * shard))
+    summed, up_sum = lax.optimization_barrier((summed, up_sum))
+    up_grad = spread_rows(up_sum)
     back = lax.all_to_all(
         summed.reshape(2, owners, SLOT_EXP, width), OWNERS, 1, 1, tiled=True
     ).reshape(2, slots, width)
     slot_out, slot_in_grad = back[0], back[1]
 
-    up_term = mul(rows_in, hidden_grad, ((0,), (0,))).astype(low)
-    up_term = up_term.reshape(4, 4, width // 16, 4 * shard)
-    up_sum = sum_hidden(up_term)
-    up_grad = lax.all_to_all(up_sum, "y", 0, 0)
-    up_grad = jnp.transpose(up_grad, (1, 0, 2)).reshape(1, width // 16, 16 * shard)
+    up_grad = up_grad.reshape(1, width // 16, 16 * shard)
 
     dcombine = mul(output_grad, slot_out, ((1,), (1,)))
     ddispatch = mul(patches, slot_in_grad, ((1,), (1,)))

time: 271 us -> 251 us (0.926)
  blocking collectives: 32.8 us -> 132 us
  waiting for transfers between devices: 94.7 us -> 22.4 us
  starting transfers between devices: 108 us -> 55.9 us
  local copies, waits for them, and re-layouts: 12.8 us -> 16.7 us
    all_gather x0 -> x2, blocking collectives: none -> 70 us  [the longest x1 43.8 us: local(): up_rows = lax.all_gather(up_weight[0].T, 'h').reshape(4 * shard, width)]
    all_to_all x1, waiting for transfers between devices: 34.9 us -> 0.01 us  [local(): lax.all_to_all(both, OWNERS, 1, 1, tiled=True).reshape(2, slots, width)]
    all_to_all x1 -> x2, blocking collectives: 32.8 us -> 62 us  [the longest x1 46 us: local(): lax.all_to_all(summed.reshape(2, owners, SLOT_EXP, width), OWNERS, 1, 1,...]
    all_to_all x3 -> x1, starting transfers between devices: 29.7 us -> 3.65 us  [local(): lax.all_to_all(parts, 'y', 0, 0).astype(jnp.float32)]
    ppermute x8 -> x7, starting transfers between devices: 41.5 us -> 27.5 us  [shift(): lax.ppermute(values, axis, [(i, (i + step) % size) for i in range(size)])]
    all_to_all x3 -> x1, waiting for transfers between devices: 13.9 us -> 0.01 us  [local(): lax.all_to_all(parts, 'y', 0, 0).astype(jnp.float32)]
    ppermute x8 -> x7, waiting for transfers between devices: 21.2 us -> 8.7 us  [shift(): lax.ppermute(values, axis, [(i, (i + step) % size) for i in range(size)])]
    all_to_all x3, starting transfers between devices: 26.1 us -> 14.4 us  [everywhere(): return lax.all_to_all(spread, axes, 0, 0)]
  transfers between devices with their start and end apart: 15 -> 12, of which waited for: 9 -> 6; matrix products, arithmetic and copies ran while one was open for 5% -> 6% of each run, Pallas kernels for 0% -> 0%
where the time goes in v4:
time: 251 us; the launch traced here: 250 us
  blocking collectives  132 us (53%)
  starting transfers between devices  55.9 us (22%)
  waiting for transfers between devices  22.4 us (9%)
  local copies, waits for them, and re-layouts  16.7 us (7%)
  matrix products  14.8 us (6%)
  other arithmetic  7.27 us (3%)
    all_to_all x1, blocking collectives, local(): lax.all_to_all(summed.reshape(2, owners, SLOT_EXP, width), OWNERS, 1, 1,...  46 us
    all_gather x1, blocking collectives, local(): up_rows = lax.all_gather(up_weight[0].T, 'h').reshape(4 * shard, width)  43.8 us
    ppermute x7, starting transfers between devices, shift(): lax.ppermute(values, axis, [(i, (i + step) % size) for i in range(size)])  27.5 us
    all_gather x1, blocking collectives, local(): down_rows = lax.all_gather(down_rows, 'h').reshape(4 * shard, width)  26.2 us
    all_to_all x1, blocking collectives, local(): lax.all_to_all(piece, ('y', 'x', 'c'), 0, 0).astype(jnp.float32)  15.9 us
    dot_general x13, matrix products, mul(): lax.dot_general(a, b, (dims, ((), ())), preferred_element_type=jnp.float32)  14.8 us
    all_to_all x3, starting transfers between devices, everywhere(): return lax.all_to_all(spread, axes, 0, 0)  14.4 us
    all_to_all x3, waiting for transfers between devices, everywhere(): return lax.all_to_all(spread, axes, 0, 0)  13.7 us
  transfers between devices with their start and end apart: 12, of which 6 were waited for; matrix products, arithmetic and copies ran while one was open for 6% of the time, Pallas kernels for 0%

profile of v4, /device:TPU:1, one launch (start us, length us, event | category | flops | bytes accessed | tf_op | source)
XLA Modules:
  0.0 250.2 jit_solution(12011749685657236948)
XLA Ops:
  5.8 10.4 %all-to-all-start = ((bf16[2,32,8,640]{3,2,0,1:T(8,128)(2,1)}), bf16[2,32,8,640]{3,2,0,1:T(8,128)(2,1)S(1)}, u32[]{:S(2)}, u32[]{:S(2)}) async-start(bf16[2,32,8,640]{3,2,0,1:T(8,128)(2,1)} %pad_maximum_fusion.1), calls=%async_computation | async-start | bytes 1310720 | tf_op jit(solution)/shard_map/all_to_all | solution.py:86
  16.2 43.8 %all-gather = bf16[640,640]{1,0:T(8,128)(2,1)} all-gather(bf16[160,640]{1,0:T(8,128)(2,1)S(1)} %bitcast.107), channel_id=2, replica_groups=mesh['y'=4,'h'=4,'x'=4,'l'=4,'c'=2] {'h'}, dimensions={0}, use_global_device_ids=true | all-gather | bytes 1024000 | tf_op jit(solution)/shard_map/all_gather | solution.py:87
  61.7 4.0 %all-to-all-start.1 = ((bf16[4,2,256,640]{3,2,1,0:T(8,128)(2,1)}), bf16[4,2,256,640]{3,2,1,0:T(8,128)(2,1)S(1)}, u32[]{:S(2)}, u32[]{:S(2)}) async-start(bf16[4,2,256,640]{3,2,1,0:T(8,128)(2,1)} %broadcast_in_dim.8), calls=%async_computation.1 | async-start | bytes 5242880 | tf_op jit(solution)/shard_map/all_to_all | solution.py:67
  65.7 26.2 %all-gather.1 = bf16[640,640]{1,0:T(8,128)(2,1)} all-gather(bf16[160,640]{1,0:T(8,128)(2,1)S(1)} %bitcast.108), channel_id=3, replica_groups=mesh['y'=4,'h'=4,'x'=4,'l'=4,'c'=2] {'h'}, dimensions={0}, use_global_device_ids=true | all-gather | bytes 1024000 | tf_op jit(solution)/shard_map/all_gather | solution.py:89
  91.9 4.8 %all-to-all-done.1 = bf16[4,2,256,640]{3,2,1,0:T(8,128)(2,1)S(1)} async-done(((bf16[4,2,256,640]{3,2,1,0:T(8,128)(2,1)}), bf16[4,2,256,640]{3,2,1,0:T(8,128)(2,1)S(1)}, u32[]{:S(2)}, u32[]{:S(2)}) %all-to-all-start.1) | async-done | bytes 2621472 | tf_op jit(solution)/shard_map/all_to_all | solution.py:67
  100.8 2.4 fusion.6
  104.6 1.8 pad_maximum_fusion
  106.3 3.7 %all-to-all-start.2 = ((bf16[4,2,256,640]{3,2,1,0:T(8,128)(2,1)}), bf16[4,2,256,640]{3,2,1,0:T(8,128)(2,1)S(1)}, u32[]{:S(2)}, u32[]{:S(2)}) async-start(bf16[4,2,256,640]{3,2,1,0:T(8,128)(2,1)} %pad_maximum_fusion), calls=%async_computation.2 | async-start | bytes 5242880 | tf_op jit(solution)/shard_map/all_to_all | solution.py:101
  110.0 2.9 %convolution_convert_fusion.2 = bf16[640,640]{1,0:T(8,128)(2,1)S(1)} fusion(bf16[1024,640]{1,0:T(8,128)(2,1)} %bitcast.98, bf16[1024,640]{1,0:T(8,128)(2,1)} %copy-done.10), kind=kOutput, calls=%fused_computation.13 | convolution fusion | flops 839270400 | bytes 3440640 | tf_op jit(solution)/shard_map/dot_general | solution.py:28
  113.0 2.8 %collective-permute-start = (bf16[2,40,640]{2,1,0:T(8,128)(2,1)S(1)}, bf16[2,40,640]{2,1,0:T(8,128)(2,1)S(1)}, u32[]{:S(2)}, u32[]{:S(2)}) collective-permute-start(bf16[2,40,640]{2,1,0:T(8,128)(2,1)S(1)} %get-tuple-element.23), channel_id=1, source_target_pairs={{0,32},{32,64},{64,96},{96,0},{1,33},{33,65},{65,97},{97,1},{2,34}... | collective-permute-start | bytes 307208 | tf_op jit(solution)/shard_map/ppermute | solution.py:33
  115.8 6.4 %collective-permute-start.2 = (bf16[2,40,640]{2,1,0:T(8,128)(2,1)S(1)}, bf16[2,40,640]{2,1,0:T(8,128)(2,1)S(1)}, u32[]{:S(2)}, u32[]{:S(2)}) collective-permute-start(bf16[2,40,640]{2,1,0:T(8,128)(2,1)S(1)} %get-tuple-element.25), channel_id=1, source_target_pairs={{0,96},{32,0},{64,32},{96,64},{1,97},{33,1},{65,33},{97,65},{2,98}... | collective-permute-start | bytes 307208 | tf_op jit(solution)/shard_map/ppermute | solution.py:33
  122.5 3.0 %collective-permute-done.2 = bf16[2,40,640]{2,1,0:T(8,128)(2,1)S(1)} collective-permute-done((bf16[2,40,640]{2,1,0:T(8,128)(2,1)S(1)}, bf16[2,40,640]{2,1,0:T(8,128)(2,1)S(1)}, u32[]{:S(2)}, u32[]{:S(2)}) %collective-permute-start.2) | collective-permute-done | bytes 102432 | tf_op jit(solution)/shard_map/ppermute | solution.py:33
  126.2 2.4 collective-permute-start.1
  129.3 6.8 %collective-permute-start.3 = (bf16[4,40,640]{2,1,0:T(8,128)(2,1)}, bf16[4,40,640]{2,1,0:T(8,128)(2,1)}, u32[]{:S(2)}, u32[]{:S(2)}) collective-permute-start(bf16[4,40,640]{2,1,0:T(8,128)(2,1)} %pad_maximum_fusion.3), channel_id=1, source_target_pairs={{0,96},{32,0},{64,32},{96,64},{1,97},{33,1},{65,33},{97,65},{2,98}... | collective-permute-start | bytes 614408 | tf_op jit(solution)/shard_map/ppermute | solution.py:33
  136.1 3.6 %collective-permute-done.1 = bf16[4,40,640]{2,1,0:T(8,128)(2,1)S(1)} collective-permute-done((bf16[4,40,640]{2,1,0:T(8,128)(2,1)}, bf16[4,40,640]{2,1,0:T(8,128)(2,1)S(1)}, u32[]{:S(2)}, u32[]{:S(2)}) %collective-permute-start.1) | collective-permute-done | bytes 204832 | tf_op jit(solution)/shard_map/ppermute | solution.py:33
  140.4 1.9 collective-permute-done.3
  146.2 46.0 %all_to_all.35 = bf16[2,32,8,640]{3,2,0,1:T(8,128)(2,1)S(1)} all-to-all(bf16[2,32,8,640]{3,2,0,1:T(8,128)(2,1)S(1)} %copy.82), channel_id=1, replica_groups=mesh['y'=4,'h'=4,'x'=4,'l'=4,'c'=2] {'x','l','c'}, dimensions={1} | all-to-all | bytes 1310720 | tf_op jit(solution)/shard_map/all_to_all | solution.py:106
  193.6 15.9 %all_to_all.36 = bf16[32,20,256]{2,1,0:T(8,128)(2,1)S(1)} all-to-all(bf16[32,20,256]{2,1,0:T(8,128)(2,1)S(1)} %reshape.66), channel_id=1, replica_groups=mesh['y'=4,'h'=4,'x'=4,'l'=4,'c'=2] {'y','x','c'}, dimensions={0} | all-to-all | bytes 655360 | tf_op jit(solution)/shard_map/all_to_all | solution.py:124
  210.3 4.7 %all-to-all-start.5 = ((bf16[16,20,256]{2,1,0:T(8,128)(2,1)}), bf16[16,20,256]{2,1,0:T(8,128)(2,1)S(1)}, u32[]{:S(2)}, u32[]{:S(2)}) async-start(bf16[16,20,256]{2,1,0:T(8,128)(2,1)} %broadcast_in_dim.9), calls=%async_computation.5 | async-start | bytes 393216 | tf_op jit(solution)/shard_map/all_to_all | solution.py:67
  215.1 2.4 collective-permute-start.4
  217.5 3.6 %collective-permute-start.5 = (bf16[1,40,640]{2,1,0:T(8,128)(2,1)S(1)}, bf16[1,40,640]{2,1,0:T(8,128)(2,1)S(1)}, u32[]{:S(2)}, u32[]{:S(2)}) collective-permute-start(bf16[1,40,640]{2,1,0:T(8,128)(2,1)S(1)} %get-tuple-element.27), channel_id=1, source_target_pairs={{0,256},{128,384},{256,0},{384,128},{1,257},{129,385},{257,1},{385... | collective-permute-start | bytes 153608 | tf_op jit(solution)/shard_map/ppermute | solution.py:33
  221.1 3.1 %collective-permute-start.6 = (bf16[1,40,640]{2,1,0:T(8,128)(2,1)S(1)}, bf16[1,40,640]{2,1,0:T(8,128)(2,1)S(1)}, u32[]{:S(2)}, u32[]{:S(2)}) collective-permute-start(bf16[1,40,640]{2,1,0:T(8,128)(2,1)S(1)} %get-tuple-element.26), channel_id=1, source_target_pairs={{0,384},{128,0},{256,128},{384,256},{1,385},{129,1},{257,129},{385... | collective-permute-start | bytes 153608 | tf_op jit(solution)/shard_map/ppermute | solution.py:33
  233.5 5.7 %all-to-all-start.6 = ((bf16[32,20,256]{2,1,0:T(8,128)(2,1)}), bf16[32,20,256]{2,1,0:T(8,128)(2,1)S(1)}, u32[]{:S(2)}, u32[]{:S(2)}) async-start(bf16[32,20,256]{2,1,0:T(8,128)(2,1)} %broadcast_in_dim.10), calls=%async_computation.6 | async-start | bytes 786432 | tf_op jit(solution)/shard_map/all_to_all | solution.py:67
  240.5 8.9 %all-to-all-done.6 = bf16[32,20,256]{2,1,0:T(8,128)(2,1)S(1)} async-done(((bf16[32,20,256]{2,1,0:T(8,128)(2,1)}), bf16[32,20,256]{2,1,0:T(8,128)(2,1)S(1)}, u32[]{:S(2)}, u32[]{:S(2)}) %all-to-all-start.6) | async-done | bytes 327712 | tf_op jit(solution)/shard_map/all_to_all | solution.py:67
  (73 shorter events, 31.8 us)
Async XLA Ops:
  0.6 1.0 copy-start
  3.1 13.1 %copy-start.8 = (bf16[1,640,160]{1,2,0:T(8,128)(2,1)S(1)}, bf16[1,640,160]{1,2,0:T(8,128)(2,1)}, u32[]{:S(2)}) copy-start(bf16[1,640,160]{1,2,0:T(8,128)(2,1)} %param.7) | copy-start | bytes 614404
  5.8 54.2 %all-to-all-start = ((bf16[2,32,8,640]{3,2,0,1:T(8,128)(2,1)}), bf16[2,32,8,640]{3,2,0,1:T(8,128)(2,1)S(1)}, u32[]{:S(2)}, u32[]{:S(2)}) async-start(bf16[2,32,8,640]{3,2,0,1:T(8,128)(2,1)} %pad_maximum_fusion.1), calls=%async_computation | async-start | bytes 1310720 | tf_op jit(solution)/shard_map/all_to_all | solution.py:86
  61.7 4.0 %copy-start.9 = (bf16[1,160,640]{2,1,0:T(8,128)(2,1)S(1)}, bf16[1,160,640]{2,1,0:T(8,128)(2,1)}, u32[]{:S(2)}) copy-start(bf16[1,160,640]{2,1,0:T(8,128)(2,1)} %param.8) | copy-start | bytes 614404
  61.7 35.0 %all-to-all-start.1 = ((bf16[4,2,256,640]{3,2,1,0:T(8,128)(2,1)}), bf16[4,2,256,640]{3,2,1,0:T(8,128)(2,1)S(1)}, u32[]{:S(2)}, u32[]{:S(2)}) async-start(bf16[4,2,256,640]{3,2,1,0:T(8,128)(2,1)} %broadcast_in_dim.8), calls=%async_computation.1 | async-start | bytes 5242880 | tf_op jit(solution)/shard_map/all_to_all | solution.py:67
  96.7 1.1 copy-start.4
  97.0 3.8 %copy-start.1 = (bf16[4,1,256,640]{3,2,1,0:T(8,128)(2,1)}, bf16[4,1,256,640]{3,2,1,0:T(8,128)(2,1)S(1)}, u32[]{:S(2)}) copy-start(bf16[4,1,256,640]{3,2,1,0:T(8,128)(2,1)S(1)} %get-tuple-element.20) | copy-start | bytes 3932164
  97.0 2.2 copy-start.5
  103.2 1.3 copy-start.10
  106.3 37.2 %all-to-all-start.2 = ((bf16[4,2,256,640]{3,2,1,0:T(8,128)(2,1)}), bf16[4,2,256,640]{3,2,1,0:T(8,128)(2,1)S(1)}, u32[]{:S(2)}, u32[]{:S(2)}) async-start(bf16[4,2,256,640]{3,2,1,0:T(8,128)(2,1)} %pad_maximum_fusion), calls=%async_computation.2 | async-start | bytes 5242880 | tf_op jit(solution)/shard_map/all_to_all | solution.py:101
  113.0 12.5 %copy-start.3 = (bf16[640,640]{1,0:T(8,128)(2,1)}, bf16[640,640]{1,0:T(8,128)(2,1)S(1)}, u32[]{:S(2)}) copy-start(bf16[640,640]{1,0:T(8,128)(2,1)S(1)} %convolution_convert_fusion.2) | copy-start | bytes 2457604
  113.0 9.4 %collective-permute-start = (bf16[2,40,640]{2,1,0:T(8,128)(2,1)S(1)}, bf16[2,40,640]{2,1,0:T(8,128)(2,1)S(1)}, u32[]{:S(2)}, u32[]{:S(2)}) collective-permute-start(bf16[2,40,640]{2,1,0:T(8,128)(2,1)S(1)} %get-tuple-element.23), channel_id=1, source_target_pairs={{0,32},{32,64},{64,96},{96,0},{1,33},{33,65},{65,97},{97,1},{2,34}... | collective-permute-start | bytes 307208 | tf_op jit(solution)/shard_map/ppermute | solution.py:33
  115.8 9.6 %collective-permute-start.2 = (bf16[2,40,640]{2,1,0:T(8,128)(2,1)S(1)}, bf16[2,40,640]{2,1,0:T(8,128)(2,1)S(1)}, u32[]{:S(2)}, u32[]{:S(2)}) collective-permute-start(bf16[2,40,640]{2,1,0:T(8,128)(2,1)S(1)} %get-tuple-element.25), channel_id=1, source_target_pairs={{0,96},{32,0},{64,32},{96,64},{1,97},{33,1},{65,33},{97,65},{2,98}... | collective-permute-start | bytes 307208 | tf_op jit(solution)/shard_map/ppermute | solution.py:33
  126.2 13.5 %collective-permute-start.1 = (bf16[4,40,640]{2,1,0:T(8,128)(2,1)}, bf16[4,40,640]{2,1,0:T(8,128)(2,1)S(1)}, u32[]{:S(2)}, u32[]{:S(2)}) collective-permute-start(bf16[4,40,640]{2,1,0:T(8,128)(2,1)} %pad_maximum_fusion.2), channel_id=1, source_target_pairs={{0,32},{32,64},{64,96},{96,0},{1,33},{33,65},{65,97},{97,1},{2,34}... | collective-permute-start | bytes 614408 | tf_op jit(solution)/shard_map/ppermute | solution.py:33
  129.3 13.0 %collective-permute-start.3 = (bf16[4,40,640]{2,1,0:T(8,128)(2,1)}, bf16[4,40,640]{2,1,0:T(8,128)(2,1)}, u32[]{:S(2)}, u32[]{:S(2)}) collective-permute-start(bf16[4,40,640]{2,1,0:T(8,128)(2,1)} %pad_maximum_fusion.3), channel_id=1, source_target_pairs={{0,96},{32,0},{64,32},{96,64},{1,97},{33,1},{65,33},{97,65},{2,98}... | collective-permute-start | bytes 614408 | tf_op jit(solution)/shard_map/ppermute | solution.py:33
  139.7 0.7 copy-start.7
  145.0 47.2 %copy-start.6 = (bf16[256,640]{1,0:T(8,128)(2,1)S(1)}, bf16[256,640]{1,0:T(8,128)(2,1)}, u32[]{:S(2)}) copy-start(bf16[256,640]{1,0:T(8,128)(2,1)} %param.9) | copy-start | bytes 983044
  210.3 22.4 %all-to-all-start.5 = ((bf16[16,20,256]{2,1,0:T(8,128)(2,1)}), bf16[16,20,256]{2,1,0:T(8,128)(2,1)S(1)}, u32[]{:S(2)}, u32[]{:S(2)}) async-start(bf16[16,20,256]{2,1,0:T(8,128)(2,1)} %broadcast_in_dim.9), calls=%async_computation.5 | async-start | bytes 393216 | tf_op jit(solution)/shard_map/all_to_all | solution.py:67
  215.1 24.3 %copy-start.2 = (bf16[640,256]{1,0:T(8,128)(2,1)S(1)}, bf16[640,256]{1,0:T(8,128)(2,1)}, u32[]{:S(2)}) copy-start(bf16[640,256]{1,0:T(8,128)(2,1)} %param.6) | copy-start | bytes 983044
  215.1 11.2 %collective-permute-start.4 = (bf16[1,40,640]{2,1,0:T(8,128)(2,1)S(1)}, bf16[1,40,640]{2,1,0:T(8,128)(2,1)S(1)}, u32[]{:S(2)}, u32[]{:S(2)}) collective-permute-start(bf16[1,40,640]{2,1,0:T(8,128)(2,1)S(1)} %get-tuple-element.28), channel_id=1, source_target_pairs={{0,128},{128,256},{256,384},{384,0},{1,129},{129,257},{257,385},{3... | collective-permute-start | bytes 153608 | tf_op jit(solution)/shard_map/ppermute | solution.py:33
  217.5 10.6 %collective-permute-start.5 = (bf16[1,40,640]{2,1,0:T(8,128)(2,1)S(1)}, bf16[1,40,640]{2,1,0:T(8,128)(2,1)S(1)}, u32[]{:S(2)}, u32[]{:S(2)}) collective-permute-start(bf16[1,40,640]{2,1,0:T(8,128)(2,1)S(1)} %get-tuple-element.27), channel_id=1, source_target_pairs={{0,256},{128,384},{256,0},{384,128},{1,257},{129,385},{257,1},{385... | collective-permute-start | bytes 153608 | tf_op jit(solution)/shard_map/ppermute | solution.py:33
  221.1 8.9 %collective-permute-start.6 = (bf16[1,40,640]{2,1,0:T(8,128)(2,1)S(1)}, bf16[1,40,640]{2,1,0:T(8,128)(2,1)S(1)}, u32[]{:S(2)}, u32[]{:S(2)}) collective-permute-start(bf16[1,40,640]{2,1,0:T(8,128)(2,1)S(1)} %get-tuple-element.26), channel_id=1, source_target_pairs={{0,384},{128,0},{256,128},{384,256},{1,385},{129,1},{257,129},{385... | collective-permute-start | bytes 153608 | tf_op jit(solution)/shard_map/ppermute | solution.py:33
  233.5 15.8 %all-to-all-start.6 = ((bf16[32,20,256]{2,1,0:T(8,128)(2,1)}), bf16[32,20,256]{2,1,0:T(8,128)(2,1)S(1)}, u32[]{:S(2)}, u32[]{:S(2)}) async-start(bf16[32,20,256]{2,1,0:T(8,128)(2,1)} %broadcast_in_dim.10), calls=%async_computation.6 | async-start | bytes 786432 | tf_op jit(solution)/shard_map/all_to_all | solution.py:67

commit v5 on v4

--- a/solution.py
+++ b/solution.py
@@ -51,15 +51,20 @@
     return total.astype(terms.dtype)
 
 
+def pair(first, second, axis=0):
+    shape = first.shape[:axis] + (2,) + first.shape[axis:]
+    both = jnp.zeros(shape, first.dtype)
+    both = lax.dynamic_update_slice_in_dim(both, jnp.expand_dims(first, axis), 0, axis)
+    return lax.dynamic_update_slice_in_dim(both, jnp.expand_dims(second, axis), 1, axis)
+
+
 def spread_rows(terms):
     here = lax.axis_index("y")
-    result = jnp.zeros(terms.shape, terms.dtype)
+    blocks = []
     for step in range(4):
-        block = lax.dynamic_index_in_dim(terms, (here + step) % 4, 0, keepdims=True)
-        if step:
-            block = shift(block, "y", step)
-        result = lax.dynamic_update_slice_in_dim(result, block, (here - step) % 4, 0)
-    return jnp.transpose(result, (1, 0, 2))
+        block = lax.dynamic_index_in_dim(terms, (here + step) % 4, 0, keepdims=False)
+        blocks.append(shift(block, "y", step) if step else block)
+    return blocks
 
 
 def everywhere(values, axes, count):
@@ -98,17 +103,18 @@
     part_out = mul(activation, down_rows, ((1,), (0,))).astype(low)
     part_in = mul(hidden_grad, up_rows, ((1,), (0,))).astype(low)
     parts = jnp.stack([part_out.reshape(4, slots, width), part_in.reshape(4, slots, width)], axis=1)
-    summed = jnp.sum(lax.all_to_all(parts, "y", 0, 0).astype(jnp.float32), axis=0).astype(low)
+    parts = lax.all_to_all(parts, "y", 0, 0).reshape(4, 2, owners, SLOT_EXP, width)
+    summed = jnp.sum(parts.astype(jnp.float32), axis=0).astype(low)
+    summed = jnp.swapaxes(summed, 0, 1)
     up_term = mul(rows_in, hidden_grad, ((0,), (0,))).astype(low)
     up_sum = sum_hidden(up_term.reshape(4, 4, width // 16, 4 * shard))
     summed, up_sum = lax.optimization_barrier((summed, up_sum))
-    up_grad = spread_rows(up_sum)
-    back = lax.all_to_all(
-        summed.reshape(2, owners, SLOT_EXP, width), OWNERS, 1, 1, tiled=True
-    ).reshape(2, slots, width)
-    slot_out, slot_in_grad = back[0], back[1]
+    up_blocks = spread_rows(up_sum)
+    back = lax.all_to_all(summed, OWNERS, 0, 0)
+    back, up_blocks = lax.optimization_barrier((back, up_blocks))
+    slot_out = back[:, 0].reshape(slots, width)
+    slot_in_grad = back[:, 1].reshape(slots, width)
 
-    up_grad = up_grad.reshape(1, width // 16, 16 * shard)
 
     dcombine = mul(output_grad, slot_out, ((1,), (1,)))
     ddispatch = mul(patches, slot_in_grad, ((1,), (1,)))
@@ -120,12 +126,18 @@
 
     phi_term = mul(patches, logit_low, ((0,), (0,))).astype(low)
     pieces = SIZES["y"] * SIZES["x"] * SIZES["c"]
-    piece = phi_term.reshape(pieces, width // pieces, slots)
+    piece = phi_term.reshape(pieces // 2, 2 * width // pieces, 2, slots // 2)
+    piece = jnp.transpose(piece, (2, 0, 1, 3)).reshape(pieces, 2 * width // pieces, slots // 2)
     piece = jnp.sum(lax.all_to_all(piece, ("y", "x", "c"), 0, 0).astype(jnp.float32), axis=0)
     piece = everywhere(piece.astype(low), ("h", "l"), SIZES["h"] * SIZES["l"])
     piece = jnp.sum(piece.astype(jnp.float32), axis=0)
+    here = lax.axis_index("y")
+    up_grad = jnp.concatenate(
+        [lax.select_n((here - source) % 4, *up_blocks) for source in range(4)], axis=1
+    )[None]
     phi_grad = everywhere(piece.astype(low), ("y", "x", "c"), pieces)
-    phi_grad = phi_grad.reshape(width, slots).astype(jnp.float32)
+    phi_grad = phi_grad.reshape(2, width, slots // 2).astype(jnp.float32)
+    phi_grad = jnp.concatenate([phi_grad[0], phi_grad[1]], axis=1)
 
     image_grad = mul(dispatch_low, slot_in_grad, ((1,), (0,)))
     image_grad = image_grad + mul(logit_low, slot_params, ((1,), (1,)))

time: 251 us -> 249 us (level)
  blocking collectives: 132 us -> 70 us
  starting transfers between devices: 55.9 us -> 92.4 us
  waiting for transfers between devices: 22.4 us -> 50.9 us
  local copies, waits for them, and re-layouts: 16.7 us -> 9.23 us
    all_to_all x2 -> x0, blocking collectives: 62 us -> none  [the longest x1 46 us: local(): lax.all_to_all(summed.reshape(2, owners, SLOT_EXP, width), OWNERS, 1, 1,...]
    all_to_all x1 -> x3, starting transfers between devices: 3.65 us -> 36.3 us  [the longest x1 26.6 us: local(): back = lax.all_to_all(summed, OWNERS, 0, 0)]
    all_to_all x1 -> x3, waiting for transfers between devices: 0.01 us -> 15.8 us  [the longest x1 9.46 us: local(): lax.all_to_all(piece, ('y', 'x', 'c'), 0, 0).astype(jnp.float32)]
    all_to_all x3, waiting for transfers between devices: 13.7 us -> 24.6 us  [everywhere(): return lax.all_to_all(spread, axes, 0, 0)]
    dynamic_update_slice x4 -> x0, local copies, waits for them, and re-layouts: 7.07 us -> none  [spread_rows(): lax.dynamic_update_slice_in_dim(result, block, (here - step) % 4, 0)]
  transfers between devices with their start and end apart: 12 -> 14, of which waited for: 6 -> 10; matrix products, arithmetic and copies ran while one was open for 6% -> 3% of each run, Pallas kernels for 0% -> 0%
where the time goes in v5:
time: 249 us; the launch traced here: 247 us
  starting transfers between devices  92.4 us (37%)
  blocking collectives  70 us (28%)
  waiting for transfers between devices  50.9 us (20%)
  matrix products  14.8 us (6%)
  local copies, waits for them, and re-layouts  9.23 us (4%)
  other arithmetic  8.84 us (4%)
    all_gather x1, blocking collectives, local(): up_rows = lax.all_gather(up_weight[0].T, 'h').reshape(4 * shard, width)  43.8 us
    ppermute x7, starting transfers between devices, shift(): lax.ppermute(values, axis, [(i, (i + step) % size) for i in range(size)])  29.6 us
    all_to_all x1, starting transfers between devices, local(): back = lax.all_to_all(summed, OWNERS, 0, 0)  26.6 us
    all_gather x1, blocking collectives, local(): down_rows = lax.all_gather(down_rows, 'h').reshape(4 * shard, width)  26.2 us
    all_to_all x3, waiting for transfers between devices, everywhere(): return lax.all_to_all(spread, axes, 0, 0)  24.6 us
    all_to_all x3, starting transfers between devices, everywhere(): return lax.all_to_all(spread, axes, 0, 0)  16.1 us
    dot_general x13, matrix products, mul(): lax.dot_general(a, b, (dims, ((), ())), preferred_element_type=jnp.float32)  14.8 us
    ppermute x7, waiting for transfers between devices, shift(): lax.ppermute(values, axis, [(i, (i + step) % size) for i in range(size)])  10.5 us
  transfers between devices with their start and end apart: 14, of which 10 were waited for; matrix products, arithmetic and copies ran while one was open for 3% of the time, Pallas kernels for 0%

profile of v5, /device:TPU:1, one launch (start us, length us, event | category | flops | bytes accessed | tf_op | source)
XLA Modules:
  0.0 247.4 jit_solution(16553000895004431746)
XLA Ops:
  5.8 10.4 %all-to-all-start = ((bf16[2,32,8,640]{3,2,0,1:T(8,128)(2,1)}), bf16[2,32,8,640]{3,2,0,1:T(8,128)(2,1)S(1)}, u32[]{:S(2)}, u32[]{:S(2)}) async-start(bf16[2,32,8,640]{3,2,0,1:T(8,128)(2,1)} %pad_maximum_fusion.1), calls=%async_computation | async-start | bytes 1310720 | tf_op jit(solution)/shard_map/all_to_all | solution.py:91
  16.2 43.8 %all-gather = bf16[640,640]{1,0:T(8,128)(2,1)} all-gather(bf16[160,640]{1,0:T(8,128)(2,1)S(1)} %bitcast.125), channel_id=2, replica_groups=mesh['y'=4,'h'=4,'x'=4,'l'=4,'c'=2] {'h'}, dimensions={0}, use_global_device_ids=true | all-gather | bytes 1024000 | tf_op jit(solution)/shard_map/all_gather | solution.py:92
  61.7 4.0 %all-to-all-start.1 = ((bf16[4,2,256,640]{3,2,1,0:T(8,128)(2,1)}), bf16[4,2,256,640]{3,2,1,0:T(8,128)(2,1)S(1)}, u32[]{:S(2)}, u32[]{:S(2)}) async-start(bf16[4,2,256,640]{3,2,1,0:T(8,128)(2,1)} %broadcast_in_dim.8), calls=%async_computation.1 | async-start | bytes 5242880 | tf_op jit(solution)/shard_map/all_to_all | solution.py:72
  65.7 26.2 %all-gather.1 = bf16[640,640]{1,0:T(8,128)(2,1)} all-gather(bf16[160,640]{1,0:T(8,128)(2,1)S(1)} %bitcast.126), channel_id=3, replica_groups=mesh['y'=4,'h'=4,'x'=4,'l'=4,'c'=2] {'h'}, dimensions={0}, use_global_device_ids=true | all-gather | bytes 1024000 | tf_op jit(solution)/shard_map/all_gather | solution.py:94
  91.9 4.8 %all-to-all-done.1 = bf16[4,2,256,640]{3,2,1,0:T(8,128)(2,1)S(1)} async-done(((bf16[4,2,256,640]{3,2,1,0:T(8,128)(2,1)}), bf16[4,2,256,640]{3,2,1,0:T(8,128)(2,1)S(1)}, u32[]{:S(2)}, u32[]{:S(2)}) %all-to-all-start.1) | async-done | bytes 2621472 | tf_op jit(solution)/shard_map/all_to_all | solution.py:72
  106.3 3.7 %all-to-all-start.2 = ((bf16[4,2,256,640]{3,2,1,0:T(8,128)(2,1)}), bf16[4,2,256,640]{3,2,1,0:T(8,128)(2,1)S(1)}, u32[]{:S(2)}, u32[]{:S(2)}) async-start(bf16[4,2,256,640]{3,2,1,0:T(8,128)(2,1)} %pad_maximum_fusion), calls=%async_computation.2 | async-start | bytes 5242880 | tf_op jit(solution)/shard_map/all_to_all | solution.py:106
  110.0 2.9 %convolution_convert_fusion.2 = bf16[640,640]{1,0:T(8,128)(2,1)S(1)} fusion(bf16[1024,640]{1,0:T(8,128)(2,1)} %bitcast.114, bf16[1024,640]{1,0:T(8,128)(2,1)} %copy-done.10), kind=kOutput, calls=%fused_computation.13 | convolution fusion | flops 839270400 | bytes 3440640 | tf_op jit(solution)/shard_map/dot_general | solution.py:28
  113.0 2.8 %collective-permute-start = (bf16[2,40,640]{2,1,0:T(8,128)(2,1)S(1)}, bf16[2,40,640]{2,1,0:T(8,128)(2,1)S(1)}, u32[]{:S(2)}, u32[]{:S(2)}) collective-permute-start(bf16[2,40,640]{2,1,0:T(8,128)(2,1)S(1)} %get-tuple-element.33), channel_id=1, source_target_pairs={{0,32},{32,64},{64,96},{96,0},{1,33},{33,65},{65,97},{97,1},{2,34}... | collective-permute-start | bytes 307208 | tf_op jit(solution)/shard_map/ppermute | solution.py:33
  115.8 6.4 %collective-permute-start.2 = (bf16[2,40,640]{2,1,0:T(8,128)(2,1)S(1)}, bf16[2,40,640]{2,1,0:T(8,128)(2,1)S(1)}, u32[]{:S(2)}, u32[]{:S(2)}) collective-permute-start(bf16[2,40,640]{2,1,0:T(8,128)(2,1)S(1)} %get-tuple-element.35), channel_id=1, source_target_pairs={{0,96},{32,0},{64,32},{96,64},{1,97},{33,1},{65,33},{97,65},{2,98}... | collective-permute-start | bytes 307208 | tf_op jit(solution)/shard_map/ppermute | solution.py:33
  122.5 3.0 %collective-permute-done.2 = bf16[2,40,640]{2,1,0:T(8,128)(2,1)S(1)} collective-permute-done((bf16[2,40,640]{2,1,0:T(8,128)(2,1)S(1)}, bf16[2,40,640]{2,1,0:T(8,128)(2,1)S(1)}, u32[]{:S(2)}, u32[]{:S(2)}) %collective-permute-start.2) | collective-permute-done | bytes 102432 | tf_op jit(solution)/shard_map/ppermute | solution.py:33
  126.2 2.4 collective-permute-start.1
  129.3 6.8 %collective-permute-start.3 = (bf16[4,40,640]{2,1,0:T(8,128)(2,1)}, bf16[4,40,640]{2,1,0:T(8,128)(2,1)}, u32[]{:S(2)}, u32[]{:S(2)}) collective-permute-start(bf16[4,40,640]{2,1,0:T(8,128)(2,1)} %pad_maximum_fusion.4), channel_id=1, source_target_pairs={{0,96},{32,0},{64,32},{96,64},{1,97},{33,1},{65,33},{97,65},{2,98}... | collective-permute-start | bytes 614408 | tf_op jit(solution)/shard_map/ppermute | solution.py:33
  136.1 3.6 %collective-permute-done.1 = bf16[4,40,640]{2,1,0:T(8,128)(2,1)S(1)} collective-permute-done((bf16[4,40,640]{2,1,0:T(8,128)(2,1)}, bf16[4,40,640]{2,1,0:T(8,128)(2,1)S(1)}, u32[]{:S(2)}, u32[]{:S(2)}) %collective-permute-start.1) | collective-permute-done | bytes 204832 | tf_op jit(solution)/shard_map/ppermute | solution.py:33
  147.0 26.6 %all-to-all-start.3 = ((bf16[32,2,8,640]{3,2,1,0:T(8,128)(2,1)}), bf16[32,2,8,640]{3,2,1,0:T(8,128)(2,1)S(1)}, u32[]{:S(2)}, u32[]{:S(2)}) async-start(bf16[32,2,8,640]{3,2,1,0:T(8,128)(2,1)} %copy.53), calls=%async_computation.3 | async-start | bytes 1310720 | tf_op jit(solution)/shard_map/all_to_all | solution.py:113
  173.8 3.7 %collective-permute-start.4 = (bf16[40,640]{1,0:T(8,128)(2,1)S(1)}, bf16[40,640]{1,0:T(8,128)(2,1)S(1)}, u32[]{:S(2)}, u32[]{:S(2)}) collective-permute-start(bf16[40,640]{1,0:T(8,128)(2,1)S(1)} %get-tuple-element.44), channel_id=1, source_target_pairs={{0,128},{128,256},{256,384},{384,0},{1,129},{129,257},{257,385},{3... | collective-permute-start | bytes 153608 | tf_op jit(solution)/shard_map/ppermute | solution.py:33
  177.4 4.3 %collective-permute-start.5 = (bf16[40,640]{1,0:T(8,128)(2,1)S(1)}, bf16[40,640]{1,0:T(8,128)(2,1)S(1)}, u32[]{:S(2)}, u32[]{:S(2)}) collective-permute-start(bf16[40,640]{1,0:T(8,128)(2,1)S(1)} %get-tuple-element.43), channel_id=1, source_target_pairs={{0,256},{128,384},{256,0},{384,128},{1,257},{129,385},{257,1},{385... | collective-permute-start | bytes 153608 | tf_op jit(solution)/shard_map/ppermute | solution.py:33
  181.7 3.3 %collective-permute-start.6 = (bf16[40,640]{1,0:T(8,128)(2,1)S(1)}, bf16[40,640]{1,0:T(8,128)(2,1)S(1)}, u32[]{:S(2)}, u32[]{:S(2)}) collective-permute-start(bf16[40,640]{1,0:T(8,128)(2,1)S(1)} %get-tuple-element.42), channel_id=1, source_target_pairs={{0,384},{128,0},{256,128},{384,256},{1,385},{129,1},{257,129},{385... | collective-permute-start | bytes 153608 | tf_op jit(solution)/shard_map/ppermute | solution.py:33
  186.9 6.3 %all-to-all-done.3 = bf16[32,2,8,640]{3,2,1,0:T(8,128)(2,1)S(1)} async-done(((bf16[32,2,8,640]{3,2,1,0:T(8,128)(2,1)}), bf16[32,2,8,640]{3,2,1,0:T(8,128)(2,1)S(1)}, u32[]{:S(2)}, u32[]{:S(2)}) %all-to-all-start.3) | async-done | bytes 655392 | tf_op jit(solution)/shard_map/all_to_all | solution.py:113
  195.4 6.0 %all-to-all-start.4 = ((bf16[32,40,128]{2,1,0:T(8,128)(2,1)}), bf16[32,40,128]{2,1,0:T(8,128)(2,1)S(1)}, u32[]{:S(2)}, u32[]{:S(2)}) async-start(bf16[32,40,128]{2,1,0:T(8,128)(2,1)} %bitcast.35), calls=%async_computation.4 | async-start | bytes 655360 | tf_op jit(solution)/shard_map/all_to_all | solution.py:131
  201.5 9.5 %all-to-all-done.4 = bf16[32,40,128]{2,1,0:T(8,128)(2,1)S(1)} async-done(((bf16[32,40,128]{2,1,0:T(8,128)(2,1)}), bf16[32,40,128]{2,1,0:T(8,128)(2,1)S(1)}, u32[]{:S(2)}, u32[]{:S(2)}) %all-to-all-start.4) | async-done | bytes 327712 | tf_op jit(solution)/shard_map/all_to_all | solution.py:131
  211.7 4.7 %all-to-all-start.5 = ((bf16[16,40,128]{2,1,0:T(8,128)(2,1)}), bf16[16,40,128]{2,1,0:T(8,128)(2,1)S(1)}, u32[]{:S(2)}, u32[]{:S(2)}) async-start(bf16[16,40,128]{2,1,0:T(8,128)(2,1)} %broadcast_in_dim.9), calls=%async_computation.5 | async-start | bytes 327680 | tf_op jit(solution)/shard_map/all_to_all | solution.py:72
  217.8 10.9 %all-to-all-done.5 = bf16[16,40,128]{2,1,0:T(8,128)(2,1)S(1)} async-done(((bf16[16,40,128]{2,1,0:T(8,128)(2,1)}), bf16[16,40,128]{2,1,0:T(8,128)(2,1)S(1)}, u32[]{:S(2)}, u32[]{:S(2)}) %all-to-all-start.5) | async-done | bytes 163872 | tf_op jit(solution)/shard_map/all_to_all | solution.py:72
  229.5 7.4 %all-to-all-start.6 = ((bf16[32,40,128]{2,1,0:T(8,128)(2,1)}), bf16[32,40,128]{2,1,0:T(8,128)(2,1)S(1)}, u32[]{:S(2)}, u32[]{:S(2)}) async-start(bf16[32,40,128]{2,1,0:T(8,128)(2,1)} %broadcast_in_dim.10), calls=%async_computation.6 | async-start | bytes 655360 | tf_op jit(solution)/shard_map/all_to_all | solution.py:72
  237.7 8.8 %all-to-all-done.6 = bf16[32,40,128]{2,1,0:T(8,128)(2,1)S(1)} async-done(((bf16[32,40,128]{2,1,0:T(8,128)(2,1)}), bf16[32,40,128]{2,1,0:T(8,128)(2,1)S(1)}, u32[]{:S(2)}, u32[]{:S(2)}) %all-to-all-start.6) | async-done | bytes 327712 | tf_op jit(solution)/shard_map/all_to_all | solution.py:72
  (69 shorter events, 33.9 us)
Async XLA Ops:
  0.6 1.0 copy-start
  3.1 13.1 %copy-start.8 = (bf16[1,640,160]{1,2,0:T(8,128)(2,1)S(1)}, bf16[1,640,160]{1,2,0:T(8,128)(2,1)}, u32[]{:S(2)}) copy-start(bf16[1,640,160]{1,2,0:T(8,128)(2,1)} %param.7) | copy-start | bytes 614404
  5.8 54.2 %all-to-all-start = ((bf16[2,32,8,640]{3,2,0,1:T(8,128)(2,1)}), bf16[2,32,8,640]{3,2,0,1:T(8,128)(2,1)S(1)}, u32[]{:S(2)}, u32[]{:S(2)}) async-start(bf16[2,32,8,640]{3,2,0,1:T(8,128)(2,1)} %pad_maximum_fusion.1), calls=%async_computation | async-start | bytes 1310720 | tf_op jit(solution)/shard_map/all_to_all | solution.py:91
  61.7 4.0 %copy-start.9 = (bf16[1,160,640]{2,1,0:T(8,128)(2,1)S(1)}, bf16[1,160,640]{2,1,0:T(8,128)(2,1)}, u32[]{:S(2)}) copy-start(bf16[1,160,640]{2,1,0:T(8,128)(2,1)} %param.8) | copy-start | bytes 614404
  61.7 35.0 %all-to-all-start.1 = ((bf16[4,2,256,640]{3,2,1,0:T(8,128)(2,1)}), bf16[4,2,256,640]{3,2,1,0:T(8,128)(2,1)S(1)}, u32[]{:S(2)}, u32[]{:S(2)}) async-start(bf16[4,2,256,640]{3,2,1,0:T(8,128)(2,1)} %broadcast_in_dim.8), calls=%async_computation.1 | async-start | bytes 5242880 | tf_op jit(solution)/shard_map/all_to_all | solution.py:72
  96.7 1.1 copy-start.4
  97.0 3.8 %copy-start.1 = (bf16[4,1,256,640]{3,2,1,0:T(8,128)(2,1)}, bf16[4,1,256,640]{3,2,1,0:T(8,128)(2,1)S(1)}, u32[]{:S(2)}) copy-start(bf16[4,1,256,640]{3,2,1,0:T(8,128)(2,1)S(1)} %get-tuple-element.30) | copy-start | bytes 3932164
  97.0 2.2 copy-start.5
  103.2 1.3 copy-start.10
  106.3 37.2 %all-to-all-start.2 = ((bf16[4,2,256,640]{3,2,1,0:T(8,128)(2,1)}), bf16[4,2,256,640]{3,2,1,0:T(8,128)(2,1)S(1)}, u32[]{:S(2)}, u32[]{:S(2)}) async-start(bf16[4,2,256,640]{3,2,1,0:T(8,128)(2,1)} %pad_maximum_fusion), calls=%async_computation.2 | async-start | bytes 5242880 | tf_op jit(solution)/shard_map/all_to_all | solution.py:106
  113.0 12.5 %copy-start.3 = (bf16[640,640]{1,0:T(8,128)(2,1)}, bf16[640,640]{1,0:T(8,128)(2,1)S(1)}, u32[]{:S(2)}) copy-start(bf16[640,640]{1,0:T(8,128)(2,1)S(1)} %convolution_convert_fusion.2) | copy-start | bytes 2457604
  113.0 9.4 %collective-permute-start = (bf16[2,40,640]{2,1,0:T(8,128)(2,1)S(1)}, bf16[2,40,640]{2,1,0:T(8,128)(2,1)S(1)}, u32[]{:S(2)}, u32[]{:S(2)}) collective-permute-start(bf16[2,40,640]{2,1,0:T(8,128)(2,1)S(1)} %get-tuple-element.33), channel_id=1, source_target_pairs={{0,32},{32,64},{64,96},{96,0},{1,33},{33,65},{65,97},{97,1},{2,34}... | collective-permute-start | bytes 307208 | tf_op jit(solution)/shard_map/ppermute | solution.py:33
  115.8 9.6 %collective-permute-start.2 = (bf16[2,40,640]{2,1,0:T(8,128)(2,1)S(1)}, bf16[2,40,640]{2,1,0:T(8,128)(2,1)S(1)}, u32[]{:S(2)}, u32[]{:S(2)}) collective-permute-start(bf16[2,40,640]{2,1,0:T(8,128)(2,1)S(1)} %get-tuple-element.35), channel_id=1, source_target_pairs={{0,96},{32,0},{64,32},{96,64},{1,97},{33,1},{65,33},{97,65},{2,98}... | collective-permute-start | bytes 307208 | tf_op jit(solution)/shard_map/ppermute | solution.py:33
  126.2 13.5 %collective-permute-start.1 = (bf16[4,40,640]{2,1,0:T(8,128)(2,1)}, bf16[4,40,640]{2,1,0:T(8,128)(2,1)S(1)}, u32[]{:S(2)}, u32[]{:S(2)}) collective-permute-start(bf16[4,40,640]{2,1,0:T(8,128)(2,1)} %pad_maximum_fusion.3), channel_id=1, source_target_pairs={{0,32},{32,64},{64,96},{96,0},{1,33},{33,65},{65,97},{97,1},{2,34}... | collective-permute-start | bytes 614408 | tf_op jit(solution)/shard_map/ppermute | solution.py:33
  129.3 13.0 %collective-permute-start.3 = (bf16[4,40,640]{2,1,0:T(8,128)(2,1)}, bf16[4,40,640]{2,1,0:T(8,128)(2,1)}, u32[]{:S(2)}, u32[]{:S(2)}) collective-permute-start(bf16[4,40,640]{2,1,0:T(8,128)(2,1)} %pad_maximum_fusion.4), channel_id=1, source_target_pairs={{0,96},{32,0},{64,32},{96,64},{1,97},{33,1},{65,33},{97,65},{2,98}... | collective-permute-start | bytes 614408 | tf_op jit(solution)/shard_map/ppermute | solution.py:33
  145.0 48.3 %copy-start.6 = (bf16[256,640]{1,0:T(8,128)(2,1)S(1)}, bf16[256,640]{1,0:T(8,128)(2,1)}, u32[]{:S(2)}) copy-start(bf16[256,640]{1,0:T(8,128)(2,1)} %param.9) | copy-start | bytes 983044
  147.0 46.2 %all-to-all-start.3 = ((bf16[32,2,8,640]{3,2,1,0:T(8,128)(2,1)}), bf16[32,2,8,640]{3,2,1,0:T(8,128)(2,1)S(1)}, u32[]{:S(2)}, u32[]{:S(2)}) async-start(bf16[32,2,8,640]{3,2,1,0:T(8,128)(2,1)} %copy.53), calls=%async_computation.3 | async-start | bytes 1310720 | tf_op jit(solution)/shard_map/all_to_all | solution.py:113
  173.8 11.3 %collective-permute-start.4 = (bf16[40,640]{1,0:T(8,128)(2,1)S(1)}, bf16[40,640]{1,0:T(8,128)(2,1)S(1)}, u32[]{:S(2)}, u32[]{:S(2)}) collective-permute-start(bf16[40,640]{1,0:T(8,128)(2,1)S(1)} %get-tuple-element.44), channel_id=1, source_target_pairs={{0,128},{128,256},{256,384},{384,0},{1,129},{129,257},{257,385},{3... | collective-permute-start | bytes 153608 | tf_op jit(solution)/shard_map/ppermute | solution.py:33
  177.4 7.6 %collective-permute-start.5 = (bf16[40,640]{1,0:T(8,128)(2,1)S(1)}, bf16[40,640]{1,0:T(8,128)(2,1)S(1)}, u32[]{:S(2)}, u32[]{:S(2)}) collective-permute-start(bf16[40,640]{1,0:T(8,128)(2,1)S(1)} %get-tuple-element.43), channel_id=1, source_target_pairs={{0,256},{128,384},{256,0},{384,128},{1,257},{129,385},{257,1},{385... | collective-permute-start | bytes 153608 | tf_op jit(solution)/shard_map/ppermute | solution.py:33
  181.7 5.2 %collective-permute-start.6 = (bf16[40,640]{1,0:T(8,128)(2,1)S(1)}, bf16[40,640]{1,0:T(8,128)(2,1)S(1)}, u32[]{:S(2)}, u32[]{:S(2)}) collective-permute-start(bf16[40,640]{1,0:T(8,128)(2,1)S(1)} %get-tuple-element.42), channel_id=1, source_target_pairs={{0,384},{128,0},{256,128},{384,256},{1,385},{129,1},{257,129},{385... | collective-permute-start | bytes 153608 | tf_op jit(solution)/shard_map/ppermute | solution.py:33
  194.3 22.4 %copy-start.2 = (bf16[640,256]{1,0:T(8,128)(2,1)S(1)}, bf16[640,256]{1,0:T(8,128)(2,1)}, u32[]{:S(2)}) copy-start(bf16[640,256]{1,0:T(8,128)(2,1)} %param.6) | copy-start | bytes 983044
  195.4 15.5 %all-to-all-start.4 = ((bf16[32,40,128]{2,1,0:T(8,128)(2,1)}), bf16[32,40,128]{2,1,0:T(8,128)(2,1)S(1)}, u32[]{:S(2)}, u32[]{:S(2)}) async-start(bf16[32,40,128]{2,1,0:T(8,128)(2,1)} %bitcast.35), calls=%async_computation.4 | async-start | bytes 655360 | tf_op jit(solution)/shard_map/all_to_all | solution.py:131
  211.7 17.0 %all-to-all-start.5 = ((bf16[16,40,128]{2,1,0:T(8,128)(2,1)}), bf16[16,40,128]{2,1,0:T(8,128)(2,1)S(1)}, u32[]{:S(2)}, u32[]{:S(2)}) async-start(bf16[16,40,128]{2,1,0:T(8,128)(2,1)} %broadcast_in_dim.9), calls=%async_computation.5 | async-start | bytes 327680 | tf_op jit(solution)/shard_map/all_to_all | solution.py:72
  229.5 17.0 %all-to-all-start.6 = ((bf16[32,40,128]{2,1,0:T(8,128)(2,1)}), bf16[32,40,128]{2,1,0:T(8,128)(2,1)S(1)}, u32[]{:S(2)}, u32[]{:S(2)}) async-start(bf16[32,40,128]{2,1,0:T(8,128)(2,1)} %broadcast_in_dim.10), calls=%async_computation.6 | async-start | bytes 655360 | tf_op jit(solution)/shard_map/all_to_all | solution.py:72
  (1 other events, 0.7 us)

commit v6 on v5

--- a/solution.py
+++ b/solution.py
@@ -51,13 +51,6 @@
     return total.astype(terms.dtype)
 
 
-def pair(first, second, axis=0):
-    shape = first.shape[:axis] + (2,) + first.shape[axis:]
-    both = jnp.zeros(shape, first.dtype)
-    both = lax.dynamic_update_slice_in_dim(both, jnp.expand_dims(first, axis), 0, axis)
-    return lax.dynamic_update_slice_in_dim(both, jnp.expand_dims(second, axis), 1, axis)
-
-
 def spread_rows(terms):
     here = lax.axis_index("y")
     blocks = []
@@ -102,11 +95,12 @@
     hidden_grad = (act_grad * gelu_slope(hidden)).astype(low)
     part_out = mul(activation, down_rows, ((1,), (0,))).astype(low)
     part_in = mul(hidden_grad, up_rows, ((1,), (0,))).astype(low)
-    parts = jnp.stack([part_out.reshape(4, slots, width), part_in.reshape(4, slots, width)], axis=1)
-    parts = lax.all_to_all(parts, "y", 0, 0).reshape(4, 2, owners, SLOT_EXP, width)
+    blocks = (4, owners, SLOT_EXP, width)
+    parts = jnp.stack([part_out.reshape(blocks), part_in.reshape(blocks)], axis=2)
+    up_term = mul(rows_in, hidden_grad, ((0,), (0,))).astype(low)
+    parts, up_term = lax.optimization_barrier((parts, up_term))
+    parts = lax.all_to_all(parts, "y", 0, 0)
     summed = jnp.sum(parts.astype(jnp.float32), axis=0).astype(low)
-    summed = jnp.swapaxes(summed, 0, 1)
-    up_term = mul(rows_in, hidden_grad, ((0,), (0,))).astype(low)
     up_sum = sum_hidden(up_term.reshape(4, 4, width // 16, 4 * shard))
     summed, up_sum = lax.optimization_barrier((summed, up_sum))
     up_blocks = spread_rows(up_sum)

time: 249 us -> 249 us (level)
  waiting for transfers between devices: 50.9 us -> 48.3 us
  transfers between devices with their start and end apart: 14 -> 14, of which waited for: 10 -> 9; matrix products, arithmetic and copies ran while one was open for 3% -> 3% of each run, Pallas kernels for 0% -> 0%
where the time goes in v6:
time: 249 us; the launch traced here: 248 us
  starting transfers between devices  93.9 us (38%)
  blocking collectives  70 us (28%)
  waiting for transfers between devices  48.3 us (19%)
  matrix products  14 us (6%)
  local copies, waits for them, and re-layouts  11.2 us (4%)
  other arithmetic  9.81 us (4%)
    all_gather x1, blocking collectives, local(): up_rows = lax.all_gather(up_weight[0].T, 'h').reshape(4 * shard, width)  43.8 us
    ppermute x7, starting transfers between devices, shift(): lax.ppermute(values, axis, [(i, (i + step) % size) for i in range(size)])  30.7 us
    all_gather x1, blocking collectives, local(): down_rows = lax.all_gather(down_rows, 'h').reshape(4 * shard, width)  26.2 us
    all_to_all x1, starting transfers between devices, local(): back = lax.all_to_all(summed, OWNERS, 0, 0)  26.1 us
    all_to_all x3, waiting for transfers between devices, everywhere(): return lax.all_to_all(spread, axes, 0, 0)  24.6 us
    all_to_all x3, starting transfers between devices, everywhere(): return lax.all_to_all(spread, axes, 0, 0)  15.9 us
    dot_general x13, matrix products, mul(): lax.dot_general(a, b, (dims, ((), ())), preferred_element_type=jnp.float32)  14 us
    all_to_all x1, starting transfers between devices, local(): lax.all_to_all(both, OWNERS, 1, 1, tiled=True).reshape(2, slots, width)  10.4 us
  transfers between devices with their start and end apart: 14, of which 9 were waited for; matrix products, arithmetic and copies ran while one was open for 3% of the time, Pallas kernels for 0%

profile of v6, /device:TPU:1, one launch (start us, length us, event | category | flops | bytes accessed | tf_op | source)
XLA Modules:
  0.0 248.3 jit_solution(2677349098910278738)
XLA Ops:
  5.8 10.4 %all-to-all-start = ((bf16[2,32,8,640]{3,2,0,1:T(8,128)(2,1)}), bf16[2,32,8,640]{3,2,0,1:T(8,128)(2,1)S(1)}, u32[]{:S(2)}, u32[]{:S(2)}) async-start(bf16[2,32,8,640]{3,2,0,1:T(8,128)(2,1)} %pad_maximum_fusion.1), calls=%async_computation | async-start | bytes 1310720 | tf_op jit(solution)/shard_map/all_to_all | solution.py:84
  16.2 43.8 %all-gather = bf16[640,640]{1,0:T(8,128)(2,1)} all-gather(bf16[160,640]{1,0:T(8,128)(2,1)S(1)} %bitcast.121), channel_id=2, replica_groups=mesh['y'=4,'h'=4,'x'=4,'l'=4,'c'=2] {'h'}, dimensions={0}, use_global_device_ids=true | all-gather | bytes 1024000 | tf_op jit(solution)/shard_map/all_gather | solution.py:85
  61.8 4.0 %all-to-all-start.1 = ((bf16[4,2,256,640]{3,2,1,0:T(8,128)(2,1)}), bf16[4,2,256,640]{3,2,1,0:T(8,128)(2,1)S(1)}, u32[]{:S(2)}, u32[]{:S(2)}) async-start(bf16[4,2,256,640]{3,2,1,0:T(8,128)(2,1)} %broadcast_in_dim.8), calls=%async_computation.1 | async-start | bytes 5242880 | tf_op jit(solution)/shard_map/all_to_all | solution.py:65
  65.7 26.2 %all-gather.1 = bf16[640,640]{1,0:T(8,128)(2,1)} all-gather(bf16[160,640]{1,0:T(8,128)(2,1)S(1)} %bitcast.122), channel_id=3, replica_groups=mesh['y'=4,'h'=4,'x'=4,'l'=4,'c'=2] {'h'}, dimensions={0}, use_global_device_ids=true | all-gather | bytes 1024000 | tf_op jit(solution)/shard_map/all_gather | solution.py:87
  92.0 4.8 %all-to-all-done.1 = bf16[4,2,256,640]{3,2,1,0:T(8,128)(2,1)S(1)} async-done(((bf16[4,2,256,640]{3,2,1,0:T(8,128)(2,1)}), bf16[4,2,256,640]{3,2,1,0:T(8,128)(2,1)S(1)}, u32[]{:S(2)}, u32[]{:S(2)}) %all-to-all-start.1) | async-done | bytes 2621472 | tf_op jit(solution)/shard_map/all_to_all | solution.py:65
  99.3 2.4 fusion.6
  108.5 3.7 %all-to-all-start.2 = ((bf16[4,32,2,8,640]{4,3,1,2,0:T(8,128)(2,1)}), bf16[4,32,2,8,640]{4,3,1,2,0:T(8,128)(2,1)S(1)}, u32[]{:S(2)}, u32[]{:S(2)}) async-start(bf16[4,32,2,8,640]{4,3,1,2,0:T(8,128)(2,1)} %pad_maximum_fusion), calls=%async_computation.2 | async-start | bytes 5242880 | tf_op jit(solution)/shard_map/all_to_all | solution.py:102
  113.3 2.8 %collective-permute-start = (bf16[2,40,640]{2,1,0:T(8,128)(2,1)S(1)}, bf16[2,40,640]{2,1,0:T(8,128)(2,1)S(1)}, u32[]{:S(2)}, u32[]{:S(2)}) collective-permute-start(bf16[2,40,640]{2,1,0:T(8,128)(2,1)S(1)} %get-tuple-element.37), channel_id=1, source_target_pairs={{0,32},{32,64},{64,96},{96,0},{1,33},{33,65},{65,97},{97,1},{2,34}... | collective-permute-start | bytes 307208 | tf_op jit(solution)/shard_map/ppermute | solution.py:33
  116.1 6.4 %collective-permute-start.2 = (bf16[2,40,640]{2,1,0:T(8,128)(2,1)S(1)}, bf16[2,40,640]{2,1,0:T(8,128)(2,1)S(1)}, u32[]{:S(2)}, u32[]{:S(2)}) collective-permute-start(bf16[2,40,640]{2,1,0:T(8,128)(2,1)S(1)} %get-tuple-element.39), channel_id=1, source_target_pairs={{0,96},{32,0},{64,32},{96,64},{1,97},{33,1},{65,33},{97,65},{2,98}... | collective-permute-start | bytes 307208 | tf_op jit(solution)/shard_map/ppermute | solution.py:33
  123.5 2.2 collective-permute-done.2
  127.4 2.7 %collective-permute-start.1 = (bf16[4,40,640]{2,1,0:T(8,128)(2,1)}, bf16[4,40,640]{2,1,0:T(8,128)(2,1)S(1)}, u32[]{:S(2)}, u32[]{:S(2)}) collective-permute-start(bf16[4,40,640]{2,1,0:T(8,128)(2,1)} %pad_maximum_fusion.3), channel_id=1, source_target_pairs={{0,32},{32,64},{64,96},{96,0},{1,33},{33,65},{65,97},{97,1},{2,34}... | collective-permute-start | bytes 614408 | tf_op jit(solution)/shard_map/ppermute | solution.py:33
  130.8 6.5 %collective-permute-start.3 = (bf16[4,40,640]{2,1,0:T(8,128)(2,1)}, bf16[4,40,640]{2,1,0:T(8,128)(2,1)}, u32[]{:S(2)}, u32[]{:S(2)}) collective-permute-start(bf16[4,40,640]{2,1,0:T(8,128)(2,1)} %pad_maximum_fusion.4), channel_id=1, source_target_pairs={{0,96},{32,0},{64,32},{96,64},{1,97},{33,1},{65,33},{97,65},{2,98}... | collective-permute-start | bytes 614408 | tf_op jit(solution)/shard_map/ppermute | solution.py:33
  137.3 3.0 %collective-permute-done.1 = bf16[4,40,640]{2,1,0:T(8,128)(2,1)S(1)} collective-permute-done((bf16[4,40,640]{2,1,0:T(8,128)(2,1)}, bf16[4,40,640]{2,1,0:T(8,128)(2,1)S(1)}, u32[]{:S(2)}, u32[]{:S(2)}) %collective-permute-start.1) | collective-permute-done | bytes 204832 | tf_op jit(solution)/shard_map/ppermute | solution.py:33
  147.5 26.1 %all-to-all-start.3 = ((bf16[32,2,8,640]{3,2,1,0:T(8,128)(2,1)}), bf16[32,2,8,640]{3,2,1,0:T(8,128)(2,1)S(1)}, u32[]{:S(2)}, u32[]{:S(2)}) async-start(bf16[32,2,8,640]{3,2,1,0:T(8,128)(2,1)} %copy.69), calls=%async_computation.3 | async-start | bytes 1310720 | tf_op jit(solution)/shard_map/all_to_all | solution.py:107
  173.7 4.8 %collective-permute-start.4 = (bf16[40,640]{1,0:T(8,128)(2,1)S(1)}, bf16[40,640]{1,0:T(8,128)(2,1)S(1)}, u32[]{:S(2)}, u32[]{:S(2)}) collective-permute-start(bf16[40,640]{1,0:T(8,128)(2,1)S(1)} %get-tuple-element.48), channel_id=1, source_target_pairs={{0,128},{128,256},{256,384},{384,0},{1,129},{129,257},{257,385},{3... | collective-permute-start | bytes 153608 | tf_op jit(solution)/shard_map/ppermute | solution.py:33
  178.5 4.3 %collective-permute-start.5 = (bf16[40,640]{1,0:T(8,128)(2,1)S(1)}, bf16[40,640]{1,0:T(8,128)(2,1)S(1)}, u32[]{:S(2)}, u32[]{:S(2)}) collective-permute-start(bf16[40,640]{1,0:T(8,128)(2,1)S(1)} %get-tuple-element.47), channel_id=1, source_target_pairs={{0,256},{128,384},{256,0},{384,128},{1,257},{129,385},{257,1},{385... | collective-permute-start | bytes 153608 | tf_op jit(solution)/shard_map/ppermute | solution.py:33
  182.8 3.3 %collective-permute-start.6 = (bf16[40,640]{1,0:T(8,128)(2,1)S(1)}, bf16[40,640]{1,0:T(8,128)(2,1)S(1)}, u32[]{:S(2)}, u32[]{:S(2)}) collective-permute-start(bf16[40,640]{1,0:T(8,128)(2,1)S(1)} %get-tuple-element.46), channel_id=1, source_target_pairs={{0,384},{128,0},{256,128},{384,256},{1,385},{129,1},{257,129},{385... | collective-permute-start | bytes 153608 | tf_op jit(solution)/shard_map/ppermute | solution.py:33
  188.0 5.2 %all-to-all-done.3 = bf16[32,2,8,640]{3,2,1,0:T(8,128)(2,1)S(1)} async-done(((bf16[32,2,8,640]{3,2,1,0:T(8,128)(2,1)}), bf16[32,2,8,640]{3,2,1,0:T(8,128)(2,1)S(1)}, u32[]{:S(2)}, u32[]{:S(2)}) %all-to-all-start.3) | async-done | bytes 655392 | tf_op jit(solution)/shard_map/all_to_all | solution.py:107
  195.4 7.1 %all-to-all-start.4 = ((bf16[32,40,128]{2,1,0:T(8,128)(2,1)}), bf16[32,40,128]{2,1,0:T(8,128)(2,1)S(1)}, u32[]{:S(2)}, u32[]{:S(2)}) async-start(bf16[32,40,128]{2,1,0:T(8,128)(2,1)} %bitcast.33), calls=%async_computation.4 | async-start | bytes 655360 | tf_op jit(solution)/shard_map/all_to_all | solution.py:125
  202.6 9.5 %all-to-all-done.4 = bf16[32,40,128]{2,1,0:T(8,128)(2,1)S(1)} async-done(((bf16[32,40,128]{2,1,0:T(8,128)(2,1)}), bf16[32,40,128]{2,1,0:T(8,128)(2,1)S(1)}, u32[]{:S(2)}, u32[]{:S(2)}) %all-to-all-start.4) | async-done | bytes 327712 | tf_op jit(solution)/shard_map/all_to_all | solution.py:125
  212.8 4.5 %all-to-all-start.5 = ((bf16[16,40,128]{2,1,0:T(8,128)(2,1)}), bf16[16,40,128]{2,1,0:T(8,128)(2,1)S(1)}, u32[]{:S(2)}, u32[]{:S(2)}) async-start(bf16[16,40,128]{2,1,0:T(8,128)(2,1)} %broadcast_in_dim.9), calls=%async_computation.5 | async-start | bytes 327680 | tf_op jit(solution)/shard_map/all_to_all | solution.py:65
  218.6 10.9 %all-to-all-done.5 = bf16[16,40,128]{2,1,0:T(8,128)(2,1)S(1)} async-done(((bf16[16,40,128]{2,1,0:T(8,128)(2,1)}), bf16[16,40,128]{2,1,0:T(8,128)(2,1)S(1)}, u32[]{:S(2)}, u32[]{:S(2)}) %all-to-all-start.5) | async-done | bytes 163872 | tf_op jit(solution)/shard_map/all_to_all | solution.py:65
  230.4 7.4 %all-to-all-start.6 = ((bf16[32,40,128]{2,1,0:T(8,128)(2,1)}), bf16[32,40,128]{2,1,0:T(8,128)(2,1)S(1)}, u32[]{:S(2)}, u32[]{:S(2)}) async-start(bf16[32,40,128]{2,1,0:T(8,128)(2,1)} %broadcast_in_dim.10), calls=%async_computation.6 | async-start | bytes 655360 | tf_op jit(solution)/shard_map/all_to_all | solution.py:65
  238.5 8.8 %all-to-all-done.6 = bf16[32,40,128]{2,1,0:T(8,128)(2,1)S(1)} async-done(((bf16[32,40,128]{2,1,0:T(8,128)(2,1)}), bf16[32,40,128]{2,1,0:T(8,128)(2,1)S(1)}, u32[]{:S(2)}, u32[]{:S(2)}) %all-to-all-start.6) | async-done | bytes 327712 | tf_op jit(solution)/shard_map/all_to_all | solution.py:65
  (63 shorter events, 36.4 us)
Async XLA Ops:
  0.6 1.0 copy-start
  3.1 13.1 %copy-start.6 = (bf16[1,640,160]{1,2,0:T(8,128)(2,1)S(1)}, bf16[1,640,160]{1,2,0:T(8,128)(2,1)}, u32[]{:S(2)}) copy-start(bf16[1,640,160]{1,2,0:T(8,128)(2,1)} %param.7) | copy-start | bytes 614404
  5.8 54.2 %all-to-all-start = ((bf16[2,32,8,640]{3,2,0,1:T(8,128)(2,1)}), bf16[2,32,8,640]{3,2,0,1:T(8,128)(2,1)S(1)}, u32[]{:S(2)}, u32[]{:S(2)}) async-start(bf16[2,32,8,640]{3,2,0,1:T(8,128)(2,1)} %pad_maximum_fusion.1), calls=%async_computation | async-start | bytes 1310720 | tf_op jit(solution)/shard_map/all_to_all | solution.py:84
  61.8 4.0 %copy-start.7 = (bf16[1,160,640]{2,1,0:T(8,128)(2,1)S(1)}, bf16[1,160,640]{2,1,0:T(8,128)(2,1)}, u32[]{:S(2)}) copy-start(bf16[1,160,640]{2,1,0:T(8,128)(2,1)} %param.8) | copy-start | bytes 614404
  61.8 35.0 %all-to-all-start.1 = ((bf16[4,2,256,640]{3,2,1,0:T(8,128)(2,1)}), bf16[4,2,256,640]{3,2,1,0:T(8,128)(2,1)S(1)}, u32[]{:S(2)}, u32[]{:S(2)}) async-start(bf16[4,2,256,640]{3,2,1,0:T(8,128)(2,1)} %broadcast_in_dim.8), calls=%async_computation.1 | async-start | bytes 5242880 | tf_op jit(solution)/shard_map/all_to_all | solution.py:65
  96.8 1.1 copy-start.2
  97.0 2.3 copy-start.3
  108.5 35.5 %all-to-all-start.2 = ((bf16[4,32,2,8,640]{4,3,1,2,0:T(8,128)(2,1)}), bf16[4,32,2,8,640]{4,3,1,2,0:T(8,128)(2,1)S(1)}, u32[]{:S(2)}, u32[]{:S(2)}) async-start(bf16[4,32,2,8,640]{4,3,1,2,0:T(8,128)(2,1)} %pad_maximum_fusion), calls=%async_computation.2 | async-start | bytes 5242880 | tf_op jit(solution)/shard_map/all_to_all | solution.py:102
  113.3 10.2 %collective-permute-start = (bf16[2,40,640]{2,1,0:T(8,128)(2,1)S(1)}, bf16[2,40,640]{2,1,0:T(8,128)(2,1)S(1)}, u32[]{:S(2)}, u32[]{:S(2)}) collective-permute-start(bf16[2,40,640]{2,1,0:T(8,128)(2,1)S(1)} %get-tuple-element.37), channel_id=1, source_target_pairs={{0,32},{32,64},{64,96},{96,0},{1,33},{33,65},{65,97},{97,1},{2,34}... | collective-permute-start | bytes 307208 | tf_op jit(solution)/shard_map/ppermute | solution.py:33
  116.1 9.6 %collective-permute-start.2 = (bf16[2,40,640]{2,1,0:T(8,128)(2,1)S(1)}, bf16[2,40,640]{2,1,0:T(8,128)(2,1)S(1)}, u32[]{:S(2)}, u32[]{:S(2)}) collective-permute-start(bf16[2,40,640]{2,1,0:T(8,128)(2,1)S(1)} %get-tuple-element.39), channel_id=1, source_target_pairs={{0,96},{32,0},{64,32},{96,64},{1,97},{33,1},{65,33},{97,65},{2,98}... | collective-permute-start | bytes 307208 | tf_op jit(solution)/shard_map/ppermute | solution.py:33
  127.4 12.9 %collective-permute-start.1 = (bf16[4,40,640]{2,1,0:T(8,128)(2,1)}, bf16[4,40,640]{2,1,0:T(8,128)(2,1)S(1)}, u32[]{:S(2)}, u32[]{:S(2)}) collective-permute-start(bf16[4,40,640]{2,1,0:T(8,128)(2,1)} %pad_maximum_fusion.3), channel_id=1, source_target_pairs={{0,32},{32,64},{64,96},{96,0},{1,33},{33,65},{65,97},{97,1},{2,34}... | collective-permute-start | bytes 614408 | tf_op jit(solution)/shard_map/ppermute | solution.py:33
  130.8 12.1 %collective-permute-start.3 = (bf16[4,40,640]{2,1,0:T(8,128)(2,1)}, bf16[4,40,640]{2,1,0:T(8,128)(2,1)}, u32[]{:S(2)}, u32[]{:S(2)}) collective-permute-start(bf16[4,40,640]{2,1,0:T(8,128)(2,1)} %pad_maximum_fusion.4), channel_id=1, source_target_pairs={{0,96},{32,0},{64,32},{96,64},{1,97},{33,1},{65,33},{97,65},{2,98}... | collective-permute-start | bytes 614408 | tf_op jit(solution)/shard_map/ppermute | solution.py:33
  140.3 0.7 copy-start.5
  145.5 47.8 %copy-start.4 = (bf16[256,640]{1,0:T(8,128)(2,1)S(1)}, bf16[256,640]{1,0:T(8,128)(2,1)}, u32[]{:S(2)}) copy-start(bf16[256,640]{1,0:T(8,128)(2,1)} %param.9) | copy-start | bytes 983044
  147.5 45.7 %all-to-all-start.3 = ((bf16[32,2,8,640]{3,2,1,0:T(8,128)(2,1)}), bf16[32,2,8,640]{3,2,1,0:T(8,128)(2,1)S(1)}, u32[]{:S(2)}, u32[]{:S(2)}) async-start(bf16[32,2,8,640]{3,2,1,0:T(8,128)(2,1)} %copy.69), calls=%async_computation.3 | async-start | bytes 1310720 | tf_op jit(solution)/shard_map/all_to_all | solution.py:107
  173.7 12.4 %collective-permute-start.4 = (bf16[40,640]{1,0:T(8,128)(2,1)S(1)}, bf16[40,640]{1,0:T(8,128)(2,1)S(1)}, u32[]{:S(2)}, u32[]{:S(2)}) collective-permute-start(bf16[40,640]{1,0:T(8,128)(2,1)S(1)} %get-tuple-element.48), channel_id=1, source_target_pairs={{0,128},{128,256},{256,384},{384,0},{1,129},{129,257},{257,385},{3... | collective-permute-start | bytes 153608 | tf_op jit(solution)/shard_map/ppermute | solution.py:33
  178.5 7.6 %collective-permute-start.5 = (bf16[40,640]{1,0:T(8,128)(2,1)S(1)}, bf16[40,640]{1,0:T(8,128)(2,1)S(1)}, u32[]{:S(2)}, u32[]{:S(2)}) collective-permute-start(bf16[40,640]{1,0:T(8,128)(2,1)S(1)} %get-tuple-element.47), channel_id=1, source_target_pairs={{0,256},{128,384},{256,0},{384,128},{1,257},{129,385},{257,1},{385... | collective-permute-start | bytes 153608 | tf_op jit(solution)/shard_map/ppermute | solution.py:33
  182.8 5.2 %collective-permute-start.6 = (bf16[40,640]{1,0:T(8,128)(2,1)S(1)}, bf16[40,640]{1,0:T(8,128)(2,1)S(1)}, u32[]{:S(2)}, u32[]{:S(2)}) collective-permute-start(bf16[40,640]{1,0:T(8,128)(2,1)S(1)} %get-tuple-element.46), channel_id=1, source_target_pairs={{0,384},{128,0},{256,128},{384,256},{1,385},{129,1},{257,129},{385... | collective-permute-start | bytes 153608 | tf_op jit(solution)/shard_map/ppermute | solution.py:33
  194.4 23.3 %copy-start.1 = (bf16[640,256]{1,0:T(8,128)(2,1)S(1)}, bf16[640,256]{1,0:T(8,128)(2,1)}, u32[]{:S(2)}) copy-start(bf16[640,256]{1,0:T(8,128)(2,1)} %param.6) | copy-start | bytes 983044
  195.4 16.6 %all-to-all-start.4 = ((bf16[32,40,128]{2,1,0:T(8,128)(2,1)}), bf16[32,40,128]{2,1,0:T(8,128)(2,1)S(1)}, u32[]{:S(2)}, u32[]{:S(2)}) async-start(bf16[32,40,128]{2,1,0:T(8,128)(2,1)} %bitcast.33), calls=%async_computation.4 | async-start | bytes 655360 | tf_op jit(solution)/shard_map/all_to_all | solution.py:125
  212.8 16.8 %all-to-all-start.5 = ((bf16[16,40,128]{2,1,0:T(8,128)(2,1)}), bf16[16,40,128]{2,1,0:T(8,128)(2,1)S(1)}, u32[]{:S(2)}, u32[]{:S(2)}) async-start(bf16[16,40,128]{2,1,0:T(8,128)(2,1)} %broadcast_in_dim.9), calls=%async_computation.5 | async-start | bytes 327680 | tf_op jit(solution)/shard_map/all_to_all | solution.py:65
  230.4 17.0 %all-to-all-start.6 = ((bf16[32,40,128]{2,1,0:T(8,128)(2,1)}), bf16[32,40,128]{2,1,0:T(8,128)(2,1)S(1)}, u32[]{:S(2)}, u32[]{:S(2)}) async-start(bf16[32,40,128]{2,1,0:T(8,128)(2,1)} %broadcast_in_dim.10), calls=%async_computation.6 | async-start | bytes 655360 | tf_op jit(solution)/shard_map/all_to_all | solution.py:65
